TPU v7x, 256 devices: a whole 4x4x8 slice. The times are simulated.
256 devices in a mesh: dp: 16 (over y, x), seq: 16 (over z, core).
Axes of the slice: x: 4, y: 4, z: 8, core: 2. Of those that a mesh axis runs over, the one named last changes fastest.
Arguments:
- loaded: float32 [16, 96, 1664], P('seq', 'dp'), may hold values from -24 to 24
- tile_rows: int32 [16, 96], P('seq', 'dp'), may hold values from 0 to 95, as said below
- bucket_ids: int32 [4], replicated, may hold values from 0 to 3, as said below
- in_weight: float32 [96, 81], replicated, may hold values from -0.625 to 0.625
- in_bias: float32 [96], replicated, may hold values from -3 to 3
- bucket_bias: float32 [4, 96], replicated, may hold values from -4 to 4
- norm_gain: float32 [96], replicated, may hold values from 0.5 to 1.5
- mid_weight: float32 [27, 96, 96], replicated, may hold values from -0.125 to 0.125
- mid_bias: float32 [96], replicated, may hold values from -3 to 3
- head_gain: float32 [96], replicated, may hold values from 0.5 to 1.5
- head_weight: float32 [16, 96], replicated, may hold values from -0.625 to 0.625
- head_bias: float32 [16], replicated, may hold values from -3 to 3
Outputs:
- latent_tokens: float32 [16, 32, 26624], P(None, 'dp', 'seq')
Inputs may be any that keep to these rules, and one draw needn't show every extreme that they name: For each frame, tile_rows[g] is a permutation of the 96 tiles. The 6 entries held by one index of dp name at most 2 tiles of any one row band (band o holds tiles 6 * o to 6 * o + 5), and in every frame some index of dp names exactly 2 tiles of some band. `bucket_ids`: clips whose numbers differ by less than 4 have different buckets; clips whose numbers differ by 4 have the same one.
All inputs are finite; a program needn't handle non-finite values.
Results may differ from a plain program's by a relative error of at most 0.0003.
Values sent between devices are 32-bit elements; how exact they have to be, the bound alone decides.
A program may use at most 128 MiB of HBM per device.

v0:
```python
import jax
import jax.numpy as jnp
from jax import lax
from jax.sharding import PartitionSpec as P

FRAMES = 4


EPSILON = 1e-06
PRECISE = lax.Precision.HIGHEST


def extended(cells, sides, width):
    for axis, dim in sides:
        count = lax.axis_size(axis)
        ends = count - 1
        head = lax.slice_in_dim(cells, 0, width, axis=dim)
        tail = lax.slice_in_dim(cells, cells.shape[dim] - width, cells.shape[dim], axis=dim)
        cells = jnp.concatenate(
            [
                lax.ppermute(tail, axis, [(i, (i + 1) % count) for i in range(ends)]),
                cells,
                lax.ppermute(head, axis, [((i + 1) % count, i) for i in range(ends)]),
            ],
            axis=dim,
        )
    return cells


def passed_along(block, axis, distance):
    devices = range(lax.axis_size(axis))
    route = [(i - distance, i) for i in devices if i - distance in devices]
    return lax.ppermute(block, axis, route)


def scaled_norm(values, scales):
    square = jnp.mean(values * values, axis=-2, keepdims=True)
    return values * lax.rsqrt(square + EPSILON) * scales[:, None]


def context(source, rim_rows, history, row_len, frame_pos):
    padded = extended(source, (("dp", 1),), rim_rows * row_len)
    layers = [padded]
    current = padded
    for earlier in range(history):
        current = passed_along(current, "seq", 1)
        layers.append(jnp.where(frame_pos > earlier, current, 0.0))
    return jnp.stack(layers[::-1], 0)


def entry_conv(stacked, weights, row_len):
    rows_out = stacked.shape[2] // row_len - 2
    cells_out = rows_out * row_len
    padded = jnp.pad(stacked, ((0, 0), (0, 0), (1, 1)))
    column = jnp.arange(cells_out) % row_len
    pieces = []
    for step_time in range(3):
        for step_row in range(3):
            for step_col in range(3):
                offset_at = step_row * row_len + step_col
                tap_slab = lax.slice_in_dim(
                    padded[step_time], offset_at, offset_at + cells_out, axis=1
                )
                if step_col == 0:
                    tap_slab = jnp.where(column > 0, tap_slab, 0.0)
                if step_col == 2:
                    tap_slab = jnp.where(column < row_len - 1, tap_slab, 0.0)
                pieces.append(tap_slab)
    columns_all = jnp.concatenate(pieces, 0)
    results = [jnp.dot(weights, columns_all, precision=PRECISE, preferred_element_type=jnp.float32)]
    return jnp.stack(results, 0)


def middle_conv(stacked, tap_weights, row_len):
    rows_out = stacked.shape[2] // row_len - 2
    cells_out = rows_out * row_len
    padded = jnp.pad(stacked, ((0, 0), (0, 0), (1, 1)))
    column = jnp.arange(cells_out) % row_len
    groups = []
    for step_col in range(3):
        running = jnp.zeros((tap_weights.shape[1], cells_out), jnp.float32)
        for step_time in range(3):
            for step_row in range(3):
                offset_at = step_row * row_len + step_col
                tap_slab = lax.slice_in_dim(
                    padded[step_time], offset_at, offset_at + cells_out, axis=1
                )
                running = running + jnp.dot(
                    tap_weights[step_time * 9 + step_row * 3 + step_col],
                    tap_slab,
                    precision=PRECISE,
                    preferred_element_type=jnp.float32,
                )
        groups.append(running)
    return (
        groups[1]
        + jnp.where(column > 0, groups[0], 0.0)
        + jnp.where(column < row_len - 1, groups[2], 0.0)
    )


def body(
    loaded,
    tile_rows,
    bucket_ids,
    in_weight,
    in_bias,
    bucket_bias,
    norm_gain,
    mid_weight,
    mid_bias,
    head_gain,
    head_weight,
    head_bias,
):
    groups_dp = lax.axis_size("dp")
    tiles_dev = loaded.shape[1]
    tile_len = loaded.shape[2]
    row_len = tile_len // 2
    rows_dev = 2 * tiles_dev // 3
    capacity = 2 * ((tiles_dev // 2 + groups_dp - 1) // groups_dp)
    position = tile_rows[0]
    owners = position // tiles_dev
    owner_hot = (owners[:, None] == jnp.arange(groups_dp)[None, :]).astype(jnp.int32)
    before = jnp.cumsum(owner_hot, axis=0) - owner_hot
    ranks = jnp.sum(before * owner_hot, axis=1)
    target = owners * capacity + ranks
    placing = target[None, :] == jnp.arange(groups_dp * capacity)[:, None]
    outgoing = jnp.dot(
        placing.astype(jnp.float32),
        loaded[0],
        precision=PRECISE,
        preferred_element_type=jnp.float32,
    )
    labels = jnp.sum(jnp.where(placing, (position % tiles_dev + 1)[None, :], 0), axis=1).astype(
        jnp.float32
    )
    arrived, arrived_labels = (
        lax.all_to_all(
            outgoing.reshape(groups_dp, capacity, tile_len),
            "dp",
            split_axis=0,
            concat_axis=0,
            tiled=True,
        ),
        lax.all_to_all(
            labels.reshape(groups_dp, capacity), "dp", split_axis=0, concat_axis=0, tiled=True
        ),
    )
    wanted = (jnp.arange(tiles_dev) + 1).astype(jnp.float32)
    picking = (arrived_labels.reshape(1, -1) == wanted[:, None]).astype(jnp.float32)
    pixels = jnp.dot(
        picking,
        arrived.reshape(-1, tile_len),
        precision=PRECISE,
        preferred_element_type=jnp.float32,
    )
    pixels = pixels.reshape(3, rows_dev * row_len)
    seq_pos = lax.axis_index("seq")
    frame_pos = seq_pos % FRAMES
    clip_now = seq_pos // FRAMES
    bucket_now = jnp.sum(jnp.where(jnp.arange(bucket_ids.shape[0]) == clip_now, bucket_ids, 0))
    bucket_row = jnp.sum(
        jnp.where((jnp.arange(bucket_bias.shape[0]) == bucket_now)[:, None], bucket_bias, 0.0),
        axis=0,
    )
    offset = (in_bias + bucket_row)[:, None]
    pixel_stack = context(pixels, 1, 2, row_len, frame_pos)
    entry_out = entry_conv(pixel_stack, in_weight, row_len)[0] + offset
    active = jax.nn.silu(scaled_norm(entry_out, norm_gain))
    active_stack = context(active, 1, 2, row_len, frame_pos)
    branch = middle_conv(active_stack, mid_weight, row_len)
    summed = entry_out + branch + mid_bias[:, None]
    latent = jax.nn.silu(scaled_norm(summed, head_gain))
    latent = (
        jnp.dot(head_weight, latent, precision=PRECISE, preferred_element_type=jnp.float32)
        + head_bias[:, None]
    )
    latent_chans = latent.shape[0]
    patches = latent.reshape(latent_chans, rows_dev // 2, 2, row_len // 2, 2).transpose(
        1, 3, 0, 2, 4
    )
    patches = patches.reshape(1, rows_dev // 2, row_len // 2 * latent_chans * 4)
    return lax.all_to_all(patches, "seq", split_axis=2, concat_axis=0, tiled=True)


def solution(mesh):
    return jax.shard_map(
        body,
        mesh=mesh,
        in_specs=(
            P("seq", "dp", None),
            P("seq", "dp"),
            P(),
            P(),
            P(),
            P(),
            P(),
            P(),
            P(),
            P(),
            P(),
            P(),
        ),
        out_specs=P(None, "dp", "seq"),
        check_vma=False,
    )
```

profile of v0, /device:TPU:9, one launch (start us, length us, event | category | flops | bytes accessed | tf_op | source)
XLA Modules:
  0.0 375.8 jit_solution(17549433647084785210)
XLA Ops:
  2.4 6.8 %all-to-all-start = ((f32[16,1,2]{2,1,0:T(1,128)}), f32[16,1,2]{2,1,0:T(1,128)S(1)}, u32[]{:S(2)}, u32[]{:S(2)}) async-start(f32[16,1,2]{2,1,0:T(1,128)} %bitcast.5), calls=%async_computation | async-start | bytes 16384 | tf_op jit(solution)/shard_map/all_to_all | solution.py:146
  12.7 2.0 all-to-all-done
  14.6 4.7 %all-to-all-start.1 = ((f32[16,2,1664]{2,1,0:T(2,128)}), f32[16,2,1664]{2,1,0:T(2,128)S(1)}, u32[]{:S(2)}, u32[]{:S(2)}) async-start(f32[16,2,1664]{2,1,0:T(2,128)} %copy.24), calls=%async_computation.1 | async-start | bytes 425984 | tf_op jit(solution)/shard_map/all_to_all | solution.py:139
  21.2 3.7 all-to-all-done.1
  25.4 4.0 %collective-permute-start.1 = (f32[3,832]{1,0:T(4,128)S(1)}, f32[3,832]{1,0:T(4,128)S(1)}, u32[]{:S(2)}, u32[]{:S(2)}) collective-permute-start(f32[3,832]{1,0:T(4,128)S(1)} %get-tuple-element.51), channel_id=1, source_target_pairs={{16,0},{32,16},{48,32},{64,48},{80,64},{96,80},{112,96},{128,112},... | collective-permute-start | bytes 29960 | tf_op jit(solution)/shard_map/ppermute | solution.py:23
  29.4 1.9 collective-permute-start
  31.4 4.5 %collective-permute-done = f32[3,832]{1,0:T(4,128)S(1)} collective-permute-done((f32[3,832]{1,0:T(4,128)S(1)}, f32[3,832]{1,0:T(4,128)S(1)}, u32[]{:S(2)}, u32[]{:S(2)}) %collective-permute-start) | collective-permute-done | bytes 10016 | tf_op jit(solution)/shard_map/ppermute | solution.py:21
  36.1 8.0 %collective-permute-start.2 = (f32[3,4992]{1,0:T(4,128)S(1)}, f32[3,4992]{1,0:T(4,128)S(1)}, u32[]{:S(2)}, u32[]{:S(2)}) collective-permute-start(f32[3,4992]{1,0:T(4,128)S(1)} %concatenate.9), channel_id=1, source_target_pairs={{0,1},{1,2},{2,3},{3,4},{4,5},{5,6},{6,7},{7,8},{8,9},{9,10},{10,1... | collective-permute-start | bytes 179720 | tf_op jit(solution)/shard_map/ppermute | solution.py:33
  44.1 1.4 collective-permute-done.2
  45.5 4.3 %collective-permute-start.3 = (f32[3,4992]{1,0:T(4,128)S(1)}, f32[3,4992]{1,0:T(4,128)S(1)}, u32[]{:S(2)}, u32[]{:S(2)}) collective-permute-start(f32[3,4992]{1,0:T(4,128)S(1)} %collective-permute-done.2), channel_id=1, source_target_pairs={{0,1},{1,2},{2,3},{3,4},{4,5},{5,6},{6,7},{7,8},{8,9},{9,10},{10,1... | collective-permute-start | bytes 179720 | tf_op jit(solution)/shard_map/ppermute | solution.py:33
  52.3 1.9 concatenate.10
  56.1 1.9 collective-permute-start.5
  58.1 3.4 collective-permute-start.4
  61.4 4.7 %collective-permute-done.5 = f32[96,832]{1,0:T(8,128)S(1)} collective-permute-done((f32[96,832]{1,0:T(8,128)S(1)}, f32[96,832]{1,0:T(8,128)S(1)}, u32[]{:S(2)}, u32[]{:S(2)}) %collective-permute-start.5) | collective-permute-done | bytes 319520 | tf_op jit(solution)/shard_map/ppermute | solution.py:23
  66.2 3.7 collective-permute-done.4
  69.9 1.7 concatenate.11
  71.7 6.1 %collective-permute-start.6 = (f32[96,4992]{1,0:T(8,128)}, f32[96,4992]{1,0:T(8,128)S(1)}, u32[]{:S(2)}, u32[]{:S(2)}) collective-permute-start(f32[96,4992]{1,0:T(8,128)} %concatenate.11), channel_id=1, source_target_pairs={{0,1},{1,2},{2,3},{3,4},{4,5},{5,6},{6,7},{7,8},{8,9},{9,10},{10,1... | collective-permute-start | bytes 5750792 | tf_op jit(solution)/shard_map/ppermute | solution.py:33
  77.7 21.3 %collective-permute-done.6 = f32[96,4992]{1,0:T(8,128)S(1)} collective-permute-done((f32[96,4992]{1,0:T(8,128)}, f32[96,4992]{1,0:T(8,128)S(1)}, u32[]{:S(2)}, u32[]{:S(2)}) %collective-permute-start.6) | collective-permute-done | bytes 1916960 | tf_op jit(solution)/shard_map/ppermute | solution.py:33
  99.1 4.3 %collective-permute-start.7 = (f32[96,4992]{1,0:T(8,128)S(1)}, f32[96,4992]{1,0:T(8,128)S(1)}, u32[]{:S(2)}, u32[]{:S(2)}) collective-permute-start(f32[96,4992]{1,0:T(8,128)S(1)} %collective-permute-done.6), channel_id=1, source_target_pairs={{0,1},{1,2},{2,3},{3,4},{4,5},{5,6},{6,7},{7,8},{8,9},{9,10},{10,1... | collective-permute-start | bytes 5750792 | tf_op jit(solution)/shard_map/ppermute | solution.py:33
  103.5 20.9 %collective-permute-done.7 = f32[96,4992]{1,0:T(8,128)S(1)} collective-permute-done((f32[96,4992]{1,0:T(8,128)S(1)}, f32[96,4992]{1,0:T(8,128)S(1)}, u32[]{:S(2)}, u32[]{:S(2)}) %collective-permute-start.7) | collective-permute-done | bytes 1916960 | tf_op jit(solution)/shard_map/ppermute | solution.py:33
  124.5 2.9 select_maximum_fusion
  128.8 1.4 fusion.16
  131.5 1.4 fusion.36
  132.9 1.4 convolution_add_fusion.7
  134.4 1.4 convolution_add_fusion.6
  135.8 1.4 convolution_add_fusion.5
  137.3 1.4 convolution_add_fusion.4
  138.7 1.4 convolution_add_fusion.3
  140.2 1.5 convolution_add_fusion.2
  141.7 1.9 convolution_add_fusion.1
  143.5 1.5 convolution_add_fusion.15
  147.6 1.5 convolution_add_fusion.12
  151.7 1.4 convolution_add_fusion.9
  153.1 1.5 convolution_add_fusion.23
  154.6 1.6 convolution_add_fusion.22
  156.3 1.5 convolution_add_fusion.21
  157.8 1.5 convolution_add_fusion.20
  159.2 1.5 convolution_add_fusion.19
  160.7 1.5 convolution_add_fusion.18
  162.2 1.5 convolution_add_fusion.17
  163.7 1.4 convolution_add_fusion.16
  166.6 1.8 multiply_reduce_fusion
  170.0 15.5 %copy.29 = f32[2,416,16,2,2]{0,4,3,2,1:T(2,128)} copy(f32[2,416,16,2,2]{2,4,1,3,0:T(2,128)S(1)} %bitcast.163) | data formatting | bytes 425984 | tf_op jit(solution)/shard_map/reshape | solution.py:183
  186.1 119.6 %reduce.6 = f32[26624,2]{1,0:T(8,128)} reduce(f32[26624,1,2]{2,1,0:T(1,128)} %bitcast.160, f32[]{:T(128)} %broadcast.202), dimensions={1}, to_apply=%bitcast.152.reduce_sub_computation | reduce | bytes 425988
  305.7 11.3 %reshape.123 = f32[16,1,3328]{2,1,0:T(1,128)S(1)} reshape(f32[26624,2]{1,0:T(8,128)} %reduce.6) | data formatting | bytes 425984
  317.1 22.6 %all_to_all.29 = f32[16,1,3328]{2,1,0:T(1,128)S(1)} all-to-all(f32[16,1,3328]{2,1,0:T(1,128)S(1)} %reshape.123), channel_id=1, replica_groups=mesh['dp'=16,'seq'=16] {'seq'}, dimensions={0} | all-to-all | bytes 425984 | tf_op jit(solution)/shard_map/all_to_all | solution.py:184
  340.9 25.6 %reshape.124 = f32[26624,1,2]{2,1,0:T(1,128)} reshape(f32[16,3328]{1,0:T(8,128)S(1)} %reduce.7) | data formatting | bytes 425984
  366.5 8.9 %copy.28 = f32[1,2,16,1664]{3,1,2,0:T(2,128)} copy(f32[1,2,16,1664]{1,3,2,0:T(8,128)} %bitcast.161) | data formatting | bytes 425984 | tf_op jit(solution)/shard_map/all_to_all | solution.py:184
  (74 shorter events, 25.4 us)
Async XLA Ops:
  0.0 54.2 %copy-start = (f32[96,81]{0,1:T(8,128)S(1)}, f32[96,81]{0,1:T(8,128)}, u32[]{:S(2)}) copy-start(f32[96,81]{0,1:T(8,128)} %param.15) | copy-start | bytes 93316
  0.0 31.3 %copy-start.4 = (f32[4,96]{1,0:T(4,128)S(1)}, f32[4,96]{1,0:T(4,128)}, u32[]{:S(2)}) copy-start(f32[4,96]{1,0:T(4,128)} %param.17) | copy-start | bytes 4612
  0.0 31.4 %copy-start.8 = (f32[96]{0:T(128)S(1)}, f32[96]{0:T(128)}, u32[]{:S(2)}) copy-start(f32[96]{0:T(128)} %param.16) | copy-start | bytes 1156
  2.4 12.2 %all-to-all-start = ((f32[16,1,2]{2,1,0:T(1,128)}), f32[16,1,2]{2,1,0:T(1,128)S(1)}, u32[]{:S(2)}, u32[]{:S(2)}) async-start(f32[16,1,2]{2,1,0:T(1,128)} %bitcast.5), calls=%async_computation | async-start | bytes 16384 | tf_op jit(solution)/shard_map/all_to_all | solution.py:146
  14.6 10.3 %all-to-all-start.1 = ((f32[16,2,1664]{2,1,0:T(2,128)}), f32[16,2,1664]{2,1,0:T(2,128)S(1)}, u32[]{:S(2)}, u32[]{:S(2)}) async-start(f32[16,2,1664]{2,1,0:T(2,128)} %copy.24), calls=%async_computation.1 | async-start | bytes 425984 | tf_op jit(solution)/shard_map/all_to_all | solution.py:139
  25.4 6.0 %collective-permute-start.1 = (f32[3,832]{1,0:T(4,128)S(1)}, f32[3,832]{1,0:T(4,128)S(1)}, u32[]{:S(2)}, u32[]{:S(2)}) collective-permute-start(f32[3,832]{1,0:T(4,128)S(1)} %get-tuple-element.51), channel_id=1, source_target_pairs={{16,0},{32,16},{48,32},{64,48},{80,64},{96,80},{112,96},{128,112},... | collective-permute-start | bytes 29960 | tf_op jit(solution)/shard_map/ppermute | solution.py:23
  29.4 6.6 %collective-permute-start = (f32[3,832]{1,0:T(4,128)S(1)}, f32[3,832]{1,0:T(4,128)S(1)}, u32[]{:S(2)}, u32[]{:S(2)}) collective-permute-start(f32[3,832]{1,0:T(4,128)S(1)} %get-tuple-element.52), channel_id=1, source_target_pairs={{0,16},{16,32},{32,48},{48,64},{64,80},{80,96},{96,112},{112,128},... | collective-permute-start | bytes 29960 | tf_op jit(solution)/shard_map/ppermute | solution.py:21
  36.1 9.4 %collective-permute-start.2 = (f32[3,4992]{1,0:T(4,128)S(1)}, f32[3,4992]{1,0:T(4,128)S(1)}, u32[]{:S(2)}, u32[]{:S(2)}) collective-permute-start(f32[3,4992]{1,0:T(4,128)S(1)} %concatenate.9), channel_id=1, source_target_pairs={{0,1},{1,2},{2,3},{3,4},{4,5},{5,6},{6,7},{7,8},{8,9},{9,10},{10,1... | collective-permute-start | bytes 179720 | tf_op jit(solution)/shard_map/ppermute | solution.py:33
  45.5 5.7 %collective-permute-start.3 = (f32[3,4992]{1,0:T(4,128)S(1)}, f32[3,4992]{1,0:T(4,128)S(1)}, u32[]{:S(2)}, u32[]{:S(2)}) collective-permute-start(f32[3,4992]{1,0:T(4,128)S(1)} %collective-permute-done.2), channel_id=1, source_target_pairs={{0,1},{1,2},{2,3},{3,4},{4,5},{5,6},{6,7},{7,8},{8,9},{9,10},{10,1... | collective-permute-start | bytes 179720 | tf_op jit(solution)/shard_map/ppermute | solution.py:33
  54.2 1.4 copy-start.6
  56.1 10.0 %collective-permute-start.5 = (f32[96,832]{1,0:T(8,128)S(1)}, f32[96,832]{1,0:T(8,128)S(1)}, u32[]{:S(2)}, u32[]{:S(2)}) collective-permute-start(f32[96,832]{1,0:T(8,128)S(1)} %get-tuple-element.10), channel_id=1, source_target_pairs={{16,0},{32,16},{48,32},{64,48},{80,64},{96,80},{112,96},{128,112},... | collective-permute-start | bytes 958472 | tf_op jit(solution)/shard_map/ppermute | solution.py:23
  58.1 11.8 %collective-permute-start.4 = (f32[96,832]{1,0:T(8,128)S(1)}, f32[96,832]{1,0:T(8,128)S(1)}, u32[]{:S(2)}, u32[]{:S(2)}) collective-permute-start(f32[96,832]{1,0:T(8,128)S(1)} %get-tuple-element.11), channel_id=1, source_target_pairs={{0,16},{16,32},{32,48},{48,64},{64,80},{80,96},{96,112},{112,128},... | collective-permute-start | bytes 958472 | tf_op jit(solution)/shard_map/ppermute | solution.py:21
  71.7 27.4 %collective-permute-start.6 = (f32[96,4992]{1,0:T(8,128)}, f32[96,4992]{1,0:T(8,128)S(1)}, u32[]{:S(2)}, u32[]{:S(2)}) collective-permute-start(f32[96,4992]{1,0:T(8,128)} %concatenate.11), channel_id=1, source_target_pairs={{0,1},{1,2},{2,3},{3,4},{4,5},{5,6},{6,7},{7,8},{8,9},{9,10},{10,1... | collective-permute-start | bytes 5750792 | tf_op jit(solution)/shard_map/ppermute | solution.py:33
  99.1 25.3 %collective-permute-start.7 = (f32[96,4992]{1,0:T(8,128)S(1)}, f32[96,4992]{1,0:T(8,128)S(1)}, u32[]{:S(2)}, u32[]{:S(2)}) collective-permute-start(f32[96,4992]{1,0:T(8,128)S(1)} %collective-permute-done.6), channel_id=1, source_target_pairs={{0,1},{1,2},{2,3},{3,4},{4,5},{5,6},{6,7},{7,8},{8,9},{9,10},{10,1... | collective-permute-start | bytes 5750792 | tf_op jit(solution)/shard_map/ppermute | solution.py:33
  103.5 21.0 %copy-start.2 = (f32[96,4992]{1,0:T(8,128)S(1)}, f32[96,4992]{1,0:T(8,128)}, u32[]{:S(2)}) copy-start(f32[96,4992]{1,0:T(8,128)} %concatenate.11) | copy-start | bytes 5750788
  127.4 1.3 copy-start.3
  165.1 1.4 copy-start.5
  166.5 1.8 copy-start.7
  166.5 1.8 copy-start.9
  166.5 1.8 copy-start.10
  366.5 8.9 %copy-start.1 = (f32[96,81]{0,1:T(8,128)S(1)}, f32[96,81]{0,1:T(8,128)}, u32[]{:S(2)}) copy-start(f32[96,81]{0,1:T(8,128)} %param.15) | copy-start | bytes 93316
where the time goes:
time: 383 us; the launch traced here: 376 us
  other arithmetic  130 us (34%)
  local copies, waits for them, and re-layouts  70.1 us (18%)
  waiting for transfers between devices  63.7 us (17%)
  starting transfers between devices  45.3 us (12%)
  matrix products  43.2 us (11%)
  blocking collectives  22.6 us (6%)
    unnamed x1, other arithmetic  120 us
    ppermute x4, waiting for transfers between devices, passed_along(): return lax.ppermute(block, axis, route)  45.1 us
    dot_general x27, matrix products, middle_conv(): jnp.dot(tap_weights[step_time * 9 + step_row * 3 + step_col], tap_slab, p...  39.3 us
    unnamed x25, local copies, waits for them, and re-layouts  38.2 us
    all_to_all x1, blocking collectives, body(): lax.all_to_all(patches, 'seq', split_axis=2, concat_axis=0, tiled=True)  22.6 us
    ppermute x4, starting transfers between devices, passed_along(): return lax.ppermute(block, axis, route)  22.6 us
    reshape x1, local copies, waits for them, and re-layouts, body(): patches = patches.reshape(1, rows_dev // 2, row_len // 2 * latent_chans * 4)  15.5 us
    all_to_all x1, local copies, waits for them, and re-layouts, body(): lax.all_to_all(patches, 'seq', split_axis=2, concat_axis=0, tiled=True)  8.91 us
  transfers between devices with their start and end apart: 10, of which 9 were waited for; matrix products, arithmetic and copies ran while one was open for 1% of the time, Pallas kernels for 0%

commit v1 on v0

v1 whole, which is shorter than its diff:
```python
import functools

import jax
import jax.numpy as jnp
from jax import lax
from jax.experimental import pallas as pl
from jax.experimental.pallas import tpu as pltpu
from jax.sharding import PartitionSpec as P

F32, BF16, I32 = jnp.float32, jnp.bfloat16, jnp.int32
MESH = pl.DeviceIdType.MESH
EPSILON = 1e-06
CH = 96
ZCH = 16
W = 832
NF = 16
FRAMES = 4
CLIPS = 4
N_DP = 16
N_SEQ = 16
COLS = W // N_SEQ
TILE = 2 * W
LANES = 256
MID_K = 9 * CH

G43 = (
    (1 / 4, 0.0, 0.0),
    (-1 / 6, -1 / 6, -1 / 6),
    (-1 / 6, 1 / 6, -1 / 6),
    (1 / 24, 1 / 12, 1 / 6),
    (1 / 24, -1 / 12, 1 / 6),
    (0.0, 0.0, 1.0),
)


def iota(shape, dim):
    return lax.broadcasted_iota(I32, shape, dim)


def dot(a, b):
    return jnp.dot(a, b, preferred_element_type=F32)


def halves(x):
    hi = x.astype(BF16)
    return hi, (x - hi.astype(F32)).astype(BF16)


def prepare(
    ids, in_weight, in_bias, bucket_bias, norm_gain, mid_weight, mid_bias, head_gain,
    head_weight, head_bias, u, we, wb, cols, off,
):
    for a in range(3):
        for d in range(3):
            taps = [mid_weight[9 * a + 3 * b + d] for b in range(3)]
            outer, inner = taps[0] + taps[2], taps[1]
            s4 = taps[0] * (1 / 24) + taps[2] * (1 / 6)
            made = (
                taps[0] * 0.25,
                (outer + inner) * (-1 / 6),
                (inner - outer) * (1 / 6),
                s4 + inner * (1 / 12),
                s4 - inner * (1 / 12),
                taps[2],
            )
            for w in range(6):
                hi, lo = halves(made[w])
                rows = pl.ds((2 - a) * CH, CH)
                u[w, rows, pl.ds(d * CH, CH)] = hi
                u[w, rows, pl.ds((3 + d) * CH, CH)] = hi
                u[w, rows, pl.ds((6 + d) * CH, CH)] = lo
    n = iota((81, LANES), 1)
    d, part, h, m = n // 72, n % 72 // 24, n % 24 // 12, n % 12
    key = 3 * d + m % 3
    row = 2 * (m // 3) + h
    first = n < 216
    k = iota((81, LANES), 0)
    whi, wlo = halves(in_weight[...])
    for re in range(6):
        b = row - re
        legal = first & (b >= 0) & (b <= 2)
        for a in range(3):
            hit = legal & (k == 27 * a + 9 * b + key)
            e01 = jnp.where(hit & (part < 2), 1.0, 0.0).astype(BF16)
            e2 = jnp.where(hit & (part == 2), 1.0, 0.0).astype(BF16)
            got = dot(whi, e01) + dot(wlo, e2)
            we[pl.ds(re * CH, CH), pl.ds(a * LANES, LANES)] = got.astype(BF16)
    lines = jnp.concatenate(
        [in_bias[...], bucket_bias[...], norm_gain[...], mid_bias[...], head_gain[...]], axis=0
    )
    table = jnp.transpose(lines)
    cols[:, 0:8] = table
    clip = iota((CH, LANES), 1) % 64 // 16
    total = jnp.broadcast_to(table[:, 0:1], (CH, LANES))
    for c in range(CLIPS):
        mine = sum(
            table[:, 1 + b : 2 + b] * jnp.where(ids[c] == b, 1.0, 0.0) for b in range(4)
        )
        total = total + jnp.where(clip == c, mine, 0.0)
    off[...] = total
    line = iota((128, ZCH), 0)
    spread = jnp.where(line % 64 // 4 == iota((128, ZCH), 1), 1.0, 0.0)
    hhi, hlo = halves(head_weight[...])
    line = iota((128, CH), 0)
    for part, piece in enumerate((hhi, hlo)):
        wide = dot(spread.astype(BF16), piece)
        for c4 in range(4):
            for r in range(2):
                q2, s = c4 // 2, c4 % 2
                keep = (line // 64 == q2) & (line % 2 == s) & (line % 4 // 2 == r)
                at = (c4 * 2 + r) * CH
                wb[pl.ds(part * 128, 128), pl.ds(at, CH)] = jnp.where(keep, wide, 0.0).astype(BF16)
    hb = jnp.sum(spread * head_bias[...], axis=1, keepdims=True)
    cols[:, 8:9] = hb[0:CH]
    cols[0:32, 9:10] = hb[CH:128]


def exchange_kernel(
    loaded, tiles, ids, in_weight, in_bias, bucket_bias, norm_gain, mid_weight, mid_bias,
    head_gain, head_weight, head_bias,
    video, u, we, wb, cols, off,
    got, picked, sent, send1, recv1, send2, recv2, own_sem,
):
    o, g = lax.axis_index("dp"), lax.axis_index("seq")
    barrier = pltpu.get_barrier_semaphore()
    for k in range(1, 16):
        pl.semaphore_signal(barrier, 1, device_id=(lax.rem(o + k, 16), g), device_id_type=MESH)
        pl.semaphore_signal(barrier, 1, device_id=(o, lax.rem(g + k, 16)), device_id_type=MESH)

    here = pl.ds(pl.multiple_of(o * 8, 8), 8)
    lane = iota((1, TILE), 1)
    numbers = jnp.full((1, TILE), -1000.0, F32)
    for j in range(6):
        numbers = jnp.where(lane == 8 * o + j, tiles[0, j].astype(F32), numbers)
    got[here, :] = jnp.concatenate([loaded[0], numbers, jnp.zeros((1, TILE), F32)], axis=0)
    pl.semaphore_wait(barrier, 30)

    first = []
    for k in range(1, 16):
        copy = pltpu.make_async_remote_copy(
            src_ref=got.at[here],
            dst_ref=got.at[here],
            send_sem=send1.at[k],
            recv_sem=recv1.at[k],
            device_id=(lax.rem(o + k, 16), g),
            device_id_type=MESH,
        )
        copy.start()
        first.append(copy)

    prepare(
        ids, in_weight, in_bias, bucket_bias, norm_gain, mid_weight, mid_bias, head_gain,
        head_weight, head_bias, u, we, wb, cols, off,
    )

    for copy in first:
        copy.wait()

    label = got[pl.ds(6, 1), 0:128]
    for l in range(1, 16):
        label = jnp.maximum(label, got[pl.ds(8 * l + 6, 1), 0:128])
    m = iota((24, 128), 0) % 12
    pg, c = m // 3, m % 3
    wanted = 6 * o + 6 * ((pg + 1) // 2 - 1) + 2 * c + (pg + 1) % 2
    hot = jnp.where(label == wanted.astype(F32), 1.0, 0.0).astype(BF16)
    hot2 = jnp.concatenate([hot, hot], axis=1)
    picked[:, 0:128] = jnp.zeros((24, 128), F32)
    picked[:, 128 + TILE :] = jnp.zeros((24, 128), F32)
    for at in range(0, TILE, 128):
        hi, lo = halves(got[:, at : at + 128])
        picked[:, 128 + at : 256 + at] = dot(hot2, jnp.concatenate([hi, lo], axis=0))

    half = lax.rem(g // FRAMES, 2) * 64
    lane = iota((8, 128), 1) - half
    inside = (lane >= 0) & (lane < 64)
    upper = iota((8, 128), 0) < 4
    for s in range(N_SEQ):
        col = lane + (COLS * s - 4)
        keep = inside & (col >= 0) & (col < W)
        pieces = []
        for h, rows in ((0, 0), (0, 8), (1, 8), (1, 16)):
            start = 128 + h * W + COLS * s - 4
            base = start // 128 * 128
            wide = picked[rows : rows + 8, base : base + 256]
            turned = pltpu.roll(wide, lax.rem(half + 256 - (start - base), 256), 1)
            pieces.append(turned[:, 0:128])
        sent[s, 0:8] = jnp.where(keep, pieces[0], 0.0)
        sent[s, 8:16] = jnp.where(keep, jnp.where(upper, pieces[1], pieces[2]), 0.0)
        sent[s, 16:24] = jnp.where(keep, pieces[3], 0.0)

    second = []
    for k in range(1, 16):
        s = lax.rem(g + k, 16)
        copy = pltpu.make_async_remote_copy(
            src_ref=sent.at[s],
            dst_ref=video.at[g],
            send_sem=send2.at[k],
            recv_sem=recv2.at[k],
            device_id=(o, s),
            device_id_type=MESH,
        )
        copy.start()
        second.append(copy)
    own = pltpu.make_async_copy(sent.at[g], video.at[g], own_sem)
    own.start()
    own.wait()
    for copy in second:
        copy.wait()


def encode_kernel(
    position, video, u, we, wb, cols, off,
    out, x3, entry, xs, sums, mixed, zs, turned,
):
    o, s = position()
    lane = iota((1, LANES), 1)
    c4, t = lane // 64, lane % 16
    col = COLS * s + 4 * (t - 1) + c4
    in_frame = jnp.where((col >= 0) & (col < W), 1.0, 0.0)
    low = iota((16, 128), 1) < 64

    low8 = iota((24, 128), 1) < 64
    lines = []
    for f in range(FRAMES):
        wide = jnp.concatenate(
            [
                jnp.where(low8, video[f], video[4 + f]),
                jnp.where(low8, video[8 + f], video[12 + f]),
            ],
            axis=1,
        )
        hi = wide.astype(BF16).astype(F32)
        lines += [hi, wide - hi]
    k = iota((LANES, LANES), 0)
    j = iota((LANES, LANES), 1)
    source = j % 64 // 16 * 64 + 4 * (j % 16) + j // 64
    permute = jnp.where(k == source, 1.0, 0.0).astype(BF16)
    placed = dot(jnp.concatenate(lines, axis=0).astype(BF16), permute)

    def shifted(v0, v1, select):
        b10, b32 = pltpu.roll(v0, 64, 1), pltpu.roll(v1, 64, 1)
        b3s, b0s = pltpu.roll(v1, 65, 1), pltpu.roll(v0, 63, 1)
        left = jnp.where(select, b3s, b10)
        middle = jnp.where(select, b10, b32)
        right = jnp.where(select, b32, b0s)
        return left, middle, right

    for f in range(FRAMES):
        block = placed[48 * f : 48 * f + 48]
        v0, v1 = block[:, 0:128], block[:, 128:256]
        left, middle, right = shifted(v0, v1, iota((48, 128), 1) < 64)
        taps = []
        for a, b in ((left, middle), (v0, v1), (middle, right)):
            both = jnp.concatenate([a, b], axis=1)
            taps += [both, both[0:24]]
        taps.append(jnp.zeros((40, LANES), F32))
        x3[pl.ds(f * LANES, LANES), :] = jnp.concatenate(taps, axis=0).astype(BF16)

    def entry_of(f):
        first = max(0, f - 2)
        k0 = (2 - (f - first)) * LANES
        entry[f] = dot(we[:, k0:], x3[pl.ds(first * LANES, (f - first + 1) * LANES), :])
        inverse = []
        for re in range(6):
            total = jnp.zeros((8, LANES), F32)
            for c in range(0, CH, 8):
                value = entry[f, pl.ds(re * CH + c, 8), :] + off[pl.ds(c, 8), :]
                entry[f, pl.ds(re * CH + c, 8), :] = value
                total = total + value * value
            mean = jnp.sum(total, axis=0, keepdims=True) * (1 / CH)
            scale = lax.rsqrt(mean + EPSILON) * in_frame
            if re == 0:
                scale = scale * jnp.where(o > 0, 1.0, 0.0)
            if re == 5:
                scale = scale * jnp.where(o < N_DP - 1, 1.0, 0.0)
            inverse.append(scale)

        def group(i, _):
            at = pl.multiple_of(i * 16, 16)
            gain = cols[pl.ds(at, 16), 5:6] * 0.5
            act = []
            for re in range(6):
                v = entry[f, pl.ds(re * CH + at, 16), :] * inverse[re] * gain
                act.append(v + v * jnp.tanh(v))
            d0, d1, d2, d3, d4, d5 = act
            a, b = d4 - 4 * d2, d3 - 4 * d1
            c, e = d4 - d2, 2 * (d3 - d1)
            made = (4 * d0 - 5 * d2 + d4, a + b, a - b, c + e, c - e, 4 * d1 - 5 * d3 + d5)
            for w in range(6):
                v0, v1 = made[w][:, 0:128], made[w][:, 128:256]
                left, middle, right = shifted(v0, v1, low)
                his, los = zip(*[halves(x) for x in (left, middle, right, v0, v1)])
                for d, (p, q) in enumerate(((0, 1), (3, 4), (1, 2))):
                    for part, source in enumerate((his, los, his)):
                        rows = pl.ds((part * 3 + d) * CH + at, 16)
                        xs[w, rows, 0:128] = source[p]
                        xs[w, rows, 128:256] = source[q]
            return 0

        lax.fori_loop(0, CH // 16, group, 0)

    def middle_of(f):
        reach = min(3, FRAMES - f)

        def step(w, _):
            y = dot(u[w, 0 : reach * CH, :], xs[w])
            for later in range(reach):
                part = y[later * CH : (later + 1) * CH]
                if f == 0 or later == 2:
                    sums[f + later, w] = part
                else:
                    sums[f + later, w] = sums[f + later, w] + part
            return 0

        lax.fori_loop(0, 6, step, 0)

    def latent_of(f):
        def group(i, totals):
            at = pl.multiple_of(i * 16, 16)
            bias = cols[pl.ds(at, 16), 6:7]
            y = [sums[f, w, pl.ds(at, 16), :] for w in range(6)]
            s12, d12, s34, d34 = y[1] + y[2], y[1] - y[2], y[3] + y[4], y[3] - y[4]
            made = (y[0] + s12 + s34, d12 + 2 * d34, s12 + 4 * s34, d12 + 8 * d34 + y[5])
            fresh = []
            for r in range(4):
                v = entry[f, pl.ds((r + 1) * CH + at, 16), :] + bias + made[r]
                mixed[r, pl.ds(at, 16), :] = v
                fresh.append(totals[r] + v * v)
            return tuple(fresh)

        zero = jnp.zeros((16, LANES), F32)
        totals = lax.fori_loop(0, CH // 16, group, (zero,) * 4)
        inverse = [
            lax.rsqrt(jnp.sum(x, axis=0, keepdims=True) * (1 / CH) + EPSILON) for x in totals
        ]
        side = pl.ds(f % 2 * 128, 128)

        def finish(i, _):
            at = pl.multiple_of(i * 16, 16)
            gain = cols[pl.ds(at, 16), 7:8] * 0.5
            act = []
            for r in range(4):
                v = mixed[r, pl.ds(at, 16), :] * inverse[r] * gain
                act.append(v + v * jnp.tanh(v))
            for r in range(2):
                for pair in range(2):
                    p0 = act[r][:, pair * 128 : pair * 128 + 128]
                    p1 = act[2 + r][:, pair * 128 : pair * 128 + 128]
                    even = jnp.where(low, p0, pltpu.roll(p1, 64, 1))
                    odd = jnp.where(low, pltpu.roll(p0, 64, 1), p1)
                    for c, x in ((2 * pair, even), (2 * pair + 1, odd)):
                        hi, lo = halves(x)
                        rows = pl.ds((c * 2 + r) * CH + at, 16)
                        zs[0, rows, side] = hi
                        zs[1, rows, side] = lo
            return 0

        lax.fori_loop(0, CH // 16, finish, 0)

    def tokens_of(f):
        both = dot(wb[...], zs[0])
        bias = jnp.concatenate([cols[:, 8:9], cols[0:32, 9:10]], axis=0)
        made = both[0:128] + both[128:256] + dot(wb[0:128], zs[1]) + bias
        turned[...] = jnp.transpose(made)
        for side in range(2):
            for clip in range(CLIPS):
                for t in range(13):
                    rows = pl.ds(side * 128 + clip * 16 + t + 1, 2, stride=64)
                    out[clip * 4 + f - 1 + side, :, pl.ds(t * 128, 128)] = turned[rows, :]

    for f in range(FRAMES):
        entry_of(f)
        middle_of(f)
        latent_of(f)
        if f % 2:
            tokens_of(f)


def shape(dims, dtype):
    return jax.ShapeDtypeStruct(dims, dtype)


MADE = (
    shape((6, 3 * CH, MID_K), BF16),
    shape((6 * CH, 3 * LANES), BF16),
    shape((256, 8 * CH), BF16),
    shape((CH, 128), F32),
    shape((CH, LANES), F32),
)
VMEM = pl.BlockSpec(memory_space=pltpu.VMEM)
SMEM = pl.BlockSpec(memory_space=pltpu.SMEM)
ENCODE_SCRATCH = [
    pltpu.VMEM((FRAMES * LANES, LANES), BF16),
    pltpu.VMEM((FRAMES, 6 * CH, LANES), F32),
    pltpu.VMEM((6, MID_K, LANES), BF16),
    pltpu.VMEM((FRAMES, 6, CH, LANES), F32),
    pltpu.VMEM((4, CH, LANES), F32),
    pltpu.VMEM((2, 8 * CH, LANES), BF16),
    pltpu.VMEM((LANES, 128), F32),
]


def where_am_i():
    return lax.axis_index("dp"), lax.axis_index("seq")


def body(
    loaded, tile_rows, bucket_ids, in_weight, in_bias, bucket_bias, norm_gain, mid_weight,
    mid_bias, head_gain, head_weight, head_bias,
):
    def line(x):
        return x.reshape(1, -1)

    video, *made = pl.pallas_call(
        exchange_kernel,
        out_shape=(shape((NF, 24, 128), F32),) + MADE,
        in_specs=[VMEM, SMEM, SMEM] + [VMEM] * 9,
        out_specs=(pl.BlockSpec(memory_space=pl.ANY),) + (VMEM,) * 5,
        scratch_shapes=[
            pltpu.VMEM((128, TILE), F32),
            pltpu.VMEM((24, TILE + 256), F32),
            pltpu.VMEM((N_SEQ, 24, 128), F32),
            pltpu.SemaphoreType.DMA((16,)),
            pltpu.SemaphoreType.DMA((16,)),
            pltpu.SemaphoreType.DMA((16,)),
            pltpu.SemaphoreType.DMA((16,)),
            pltpu.SemaphoreType.DMA,
        ],
        compiler_params=pltpu.CompilerParams(
            collective_id=0, has_side_effects=True, vmem_limit_bytes=40 * 2**20
        ),
    )(
        loaded, tile_rows, bucket_ids, in_weight, line(in_bias), bucket_bias, line(norm_gain),
        mid_weight, line(mid_bias), line(head_gain), head_weight, line(head_bias),
    )
    return pl.pallas_call(
        functools.partial(encode_kernel, where_am_i),
        out_shape=shape((NF, 2, TILE), F32),
        in_specs=[VMEM] * 6,
        out_specs=VMEM,
        scratch_shapes=ENCODE_SCRATCH,
        compiler_params=pltpu.CompilerParams(vmem_limit_bytes=48 * 2**20),
    )(video, *made)


def solution(mesh):
    return jax.shard_map(
        body,
        mesh=mesh,
        in_specs=(P("seq", "dp", None), P("seq", "dp")) + (P(),) * 10,
        out_specs=P(None, "dp", "seq"),
        check_vma=False,
    )
```

time: 383 us -> 59.9 us (0.16)
  the two profiles are of different devices: /device:TPU:9 before, /device:TPU:1 now
where the time goes in v1:
time: 59.9 us; the launch traced here: 59.6 us
  Pallas kernels  50.6 us (84%)
  local copies, waits for them, and re-layouts  8.94 us (15%)
    pallas_call x1, Pallas kernels, body(): pl.pallas_call(exchange_kernel, out_shape=(shape((NF, 24, 128), F32),) +...  29.6 us
    pallas_call x1, Pallas kernels, body(): pl.pallas_call(functools.partial(encode_kernel, where_am_i), out_shape=sh...  21 us
    unnamed x22, local copies, waits for them, and re-layouts  8.94 us

profile of v1, /device:TPU:1, one launch (start us, length us, event | category | flops | bytes accessed | tf_op | source)
XLA Modules:
  0.0 59.6 jit_solution(9806819165027587353)
XLA Ops:
  0.0 0.9 %copy.14.in_weight = f32[96,81]{1,0:T(8,128)S(1)} copy(f32[96,81]{0,1:T(8,128)} %param.15) | data formatting | bytes 62208 | tf_op args[3]
  0.9 0.8 %copy.13.loaded = f32[1,6,1664]{2,1,0:T(8,128)S(1)} copy(f32[1,6,1664]{2,0,1:T(1,128)} %param.12) | data formatting | bytes 79872 | tf_op args[0]
  1.7 0.0 copy-start
  1.7 1.3 %copy-done = f32[27,96,96]{2,1,0:T(8,128)S(1)} copy-done((f32[27,96,96]{2,1,0:T(8,128)S(1)}, f32[27,96,96]{2,1,0:T(8,128)}, u32[]{:S(2)}) %copy-start) | copy-done | bytes 995352
  3.0 0.0 copy-start.1
  3.0 0.7 %copy-done.1 = f32[16,96]{1,0:T(8,128)S(1)} copy-done((f32[16,96]{1,0:T(8,128)S(1)}, f32[16,96]{1,0:T(8,128)}, u32[]{:S(2)}) %copy-start.1) | copy-done | bytes 6168
  3.7 0.0 copy-start.2
  3.7 0.7 %copy-done.2 = f32[4,96]{1,0:T(4,128)S(1)} copy-done((f32[4,96]{1,0:T(4,128)S(1)}, f32[4,96]{1,0:T(4,128)}, u32[]{:S(2)}) %copy-start.2) | copy-done | bytes 1560
  4.4 0.0 copy-start.3
  4.4 0.7 %copy-done.3 = s32[1,6]{1,0:T(1,128)S(1)} copy-done((s32[1,6]{1,0:T(1,128)S(1)}, s32[1,6]{1,0:T(1,128)}, u32[]{:S(2)}) %copy-start.3) | copy-done | bytes 48
  5.0 0.0 copy-start.4
  5.0 0.7 %copy-done.4 = s32[4]{0:T(128)S(1)} copy-done((s32[4]{0:T(128)S(1)}, s32[4]{0:T(128)}, u32[]{:S(2)}) %copy-start.4) | copy-done | bytes 40
  5.7 0.0 copy-start.5
  5.7 0.7 %copy-done.5 = f32[96]{0:T(128)S(1)} copy-done((f32[96]{0:T(128)S(1)}, f32[96]{0:T(128)}, u32[]{:S(2)}) %copy-start.5) | copy-done | bytes 408
  6.3 0.0 copy-start.6
  6.3 0.7 %copy-done.6 = f32[96]{0:T(128)S(1)} copy-done((f32[96]{0:T(128)S(1)}, f32[96]{0:T(128)}, u32[]{:S(2)}) %copy-start.6) | copy-done | bytes 408
  7.0 0.0 copy-start.7
  7.0 0.7 %copy-done.7 = f32[96]{0:T(128)S(1)} copy-done((f32[96]{0:T(128)S(1)}, f32[96]{0:T(128)}, u32[]{:S(2)}) %copy-start.7) | copy-done | bytes 408
  7.6 0.0 copy-start.8
  7.6 0.7 %copy-done.8 = f32[96]{0:T(128)S(1)} copy-done((f32[96]{0:T(128)S(1)}, f32[96]{0:T(128)}, u32[]{:S(2)}) %copy-start.8) | copy-done | bytes 408
  8.3 0.0 copy-start.9
  8.3 0.7 %copy-done.9 = f32[16]{0:T(128)S(1)} copy-done((f32[16]{0:T(128)S(1)}, f32[16]{0:T(128)}, u32[]{:S(2)}) %copy-start.9) | copy-done | bytes 88
  9.0 29.6 %shard_map.118 = (f32[16,24,128]{2,1,0:T(8,128)S(1)}, bf16[6,288,864]{2,1,0:T(8,128)(2,1)S(1)}, bf16[576,768]{1,0:T(8,128)(2,1)S(1)}, bf16[256,768]{1,0:T(8,128)...) custom-call(f32[1,6,1664]{2,1,0:T(8,128)S(1)} %copy.13.loaded, s32[1,6]{1,0:T(1,128)S(1)} %copy-done.3, ...), custom_call_target="tpu_custom_call" | custom-call | tf_op jit(solution)/shard_map/pallas_call | solution.py:414
  38.6 21.0 %shard_map.119 = f32[16,2,1664]{2,1,0:T(2,128)} custom-call(f32[16,24,128]{2,1,0:T(8,128)S(1)} %get-tuple-element.11.video, bf16[6,288,864]{2,1,0:T(8,128)(2,1)S(1)} %get-tuple-element.12.u, bf16[576,768]{1,0:T(8,128)(2,1)S(1)} %get-tuple-element.13.we, bf16[256,768]{1,0:T(8,128)(2,1)S(1)} %get-tuple-element.14.wb, f32[96,128]{1,0:T(8,128)S(1)} %get-tuple-element.15.cols, ...), custom_call_target="tpu_custom_call" | custom-call | tf_op jit(solution)/shard_map/pallas_call | solution.py:436
Async XLA Ops:
  1.7 1.3 %copy-start = (f32[27,96,96]{2,1,0:T(8,128)S(1)}, f32[27,96,96]{2,1,0:T(8,128)}, u32[]{:S(2)}) copy-start(f32[27,96,96]{2,1,0:T(8,128)} %mid_weight.1) | copy-start | bytes 2985988
  3.0 0.7 %copy-start.1 = (f32[16,96]{1,0:T(8,128)S(1)}, f32[16,96]{1,0:T(8,128)}, u32[]{:S(2)}) copy-start(f32[16,96]{1,0:T(8,128)} %head_weight.1) | copy-start | bytes 18436
  3.7 0.7 %copy-start.2 = (f32[4,96]{1,0:T(4,128)S(1)}, f32[4,96]{1,0:T(4,128)}, u32[]{:S(2)}) copy-start(f32[4,96]{1,0:T(4,128)} %bucket_bias.1) | copy-start | bytes 4612
  4.4 0.7 %copy-start.3 = (s32[1,6]{1,0:T(1,128)S(1)}, s32[1,6]{1,0:T(1,128)}, u32[]{:S(2)}) copy-start(s32[1,6]{1,0:T(1,128)} %tiles.1) | copy-start | bytes 76
  5.0 0.7 %copy-start.4 = (s32[4]{0:T(128)S(1)}, s32[4]{0:T(128)}, u32[]{:S(2)}) copy-start(s32[4]{0:T(128)} %ids.1) | copy-start | bytes 52
  5.7 0.7 %copy-start.5 = (f32[96]{0:T(128)S(1)}, f32[96]{0:T(128)}, u32[]{:S(2)}) copy-start(f32[96]{0:T(128)} %param.16) | copy-start | bytes 1156
  6.3 0.7 %copy-start.6 = (f32[96]{0:T(128)S(1)}, f32[96]{0:T(128)}, u32[]{:S(2)}) copy-start(f32[96]{0:T(128)} %param.18) | copy-start | bytes 1156
  7.0 0.7 %copy-start.7 = (f32[96]{0:T(128)S(1)}, f32[96]{0:T(128)}, u32[]{:S(2)}) copy-start(f32[96]{0:T(128)} %param.20) | copy-start | bytes 1156
  7.6 0.7 %copy-start.8 = (f32[96]{0:T(128)S(1)}, f32[96]{0:T(128)}, u32[]{:S(2)}) copy-start(f32[96]{0:T(128)} %param.21) | copy-start | bytes 1156
  8.3 0.7 %copy-start.9 = (f32[16]{0:T(128)S(1)}, f32[16]{0:T(128)}, u32[]{:S(2)}) copy-start(f32[16]{0:T(128)} %param.23) | copy-start | bytes 196

commit v2 on v1

--- a/solution.py
+++ b/solution.py
@@ -48,7 +48,7 @@
 
 def prepare(
     ids, in_weight, in_bias, bucket_bias, norm_gain, mid_weight, mid_bias, head_gain,
-    head_weight, head_bias, u, we, wb, cols, off,
+    head_weight, head_bias, u, we, wb, cols, off, end,
 ):
     for a in range(3):
         for d in range(3):
@@ -75,7 +75,7 @@
     row = 2 * (m // 3) + h
     first = n < 216
     k = iota((81, LANES), 0)
-    whi, wlo = halves(in_weight[...])
+    whi, wlo = halves(jnp.transpose(in_weight[...]))
     for re in range(6):
         b = row - re
         legal = first & (b >= 0) & (b <= 2)
@@ -89,7 +89,8 @@
         [in_bias[...], bucket_bias[...], norm_gain[...], mid_bias[...], head_gain[...]], axis=0
     )
     table = jnp.transpose(lines)
-    cols[:, 0:8] = table
+    for i, (at, scale) in enumerate(((5, 0.5), (6, 1.0), (7, 0.5))):
+        cols[i] = jnp.broadcast_to(table[:, at : at + 1] * scale, (CH, 128))
     clip = iota((CH, LANES), 1) % 64 // 16
     total = jnp.broadcast_to(table[:, 0:1], (CH, LANES))
     for c in range(CLIPS):
@@ -111,28 +112,46 @@
                 at = (c4 * 2 + r) * CH
                 wb[pl.ds(part * 128, 128), pl.ds(at, CH)] = jnp.where(keep, wide, 0.0).astype(BF16)
     hb = jnp.sum(spread * head_bias[...], axis=1, keepdims=True)
-    cols[:, 8:9] = hb[0:CH]
-    cols[0:32, 9:10] = hb[CH:128]
+    end[...] = jnp.broadcast_to(hb, (128, 128))
 
 
 def exchange_kernel(
-    loaded, tiles, ids, in_weight, in_bias, bucket_bias, norm_gain, mid_weight, mid_bias,
+    loaded, tile_rows, bucket_ids, in_weight, in_bias, bucket_bias, norm_gain, mid_weight, mid_bias,
     head_gain, head_weight, head_bias,
-    video, u, we, wb, cols, off,
+    video, u, we, wb, cols, off, end,
+    raw, numbers_smem, ids, weight_in, bias_in, buckets, gain1, weight_mid, bias_mid, gain2,
+    weight_head, bias_head, in_sems,
     got, picked, sent, send1, recv1, send2, recv2, own_sem,
 ):
     o, g = lax.axis_index("dp"), lax.axis_index("seq")
+    sources = (
+        loaded, tile_rows, bucket_ids, in_weight, in_bias, bucket_bias, norm_gain, mid_weight,
+        mid_bias, head_gain, head_weight, head_bias,
+    )
+    targets = (
+        raw, numbers_smem, ids, weight_in, bias_in, buckets, gain1, weight_mid, bias_mid, gain2,
+        weight_head, bias_head,
+    )
+    loads = [
+        pltpu.make_async_copy(a, b, in_sems.at[i]) for i, (a, b) in enumerate(zip(sources, targets))
+    ]
+    for load in loads:
+        load.start()
     barrier = pltpu.get_barrier_semaphore()
     for k in range(1, 16):
         pl.semaphore_signal(barrier, 1, device_id=(lax.rem(o + k, 16), g), device_id_type=MESH)
         pl.semaphore_signal(barrier, 1, device_id=(o, lax.rem(g + k, 16)), device_id_type=MESH)
 
+    loads[0].wait()
+    loads[1].wait()
     here = pl.ds(pl.multiple_of(o * 8, 8), 8)
     lane = iota((1, TILE), 1)
     numbers = jnp.full((1, TILE), -1000.0, F32)
     for j in range(6):
-        numbers = jnp.where(lane == 8 * o + j, tiles[0, j].astype(F32), numbers)
-    got[here, :] = jnp.concatenate([loaded[0], numbers, jnp.zeros((1, TILE), F32)], axis=0)
+        numbers = jnp.where(lane == 8 * o + j, numbers_smem[0, j].astype(F32), numbers)
+    got[here, :] = jnp.concatenate(
+        [raw[j] for j in range(6)] + [numbers, jnp.zeros((1, TILE), F32)], axis=0
+    )
     pl.semaphore_wait(barrier, 30)
 
     first = []
@@ -148,9 +167,11 @@
         copy.start()
         first.append(copy)
 
+    for load in loads[2:]:
+        load.wait()
     prepare(
-        ids, in_weight, in_bias, bucket_bias, norm_gain, mid_weight, mid_bias, head_gain,
-        head_weight, head_bias, u, we, wb, cols, off,
+        ids, weight_in, bias_in, buckets, gain1, weight_mid, bias_mid, gain2, weight_head,
+        bias_head, u, we, wb, cols, off, end,
     )
 
     for copy in first:
@@ -209,7 +230,7 @@
 
 
 def encode_kernel(
-    position, video, u, we, wb, cols, off,
+    position, video, u, we, wb, cols, off, end,
     out, x3, entry, xs, sums, mixed, zs, turned,
 ):
     o, s = position()
@@ -236,6 +257,10 @@
     source = j % 64 // 16 * 64 + 4 * (j % 16) + j // 64
     permute = jnp.where(k == source, 1.0, 0.0).astype(BF16)
     placed = dot(jnp.concatenate(lines, axis=0).astype(BF16), permute)
+
+    def wide_column(which, at):
+        column = cols[which, pl.ds(at, 16), :]
+        return jnp.concatenate([column, column], axis=1)
 
     def shifted(v0, v1, select):
         b10, b32 = pltpu.roll(v0, 64, 1), pltpu.roll(v1, 64, 1)
@@ -276,8 +301,8 @@
             inverse.append(scale)
 
         def group(i, _):
-            at = pl.multiple_of(i * 16, 16)
-            gain = cols[pl.ds(at, 16), 5:6] * 0.5
+            at = i * 16
+            gain = wide_column(0, at)
             act = []
             for re in range(6):
                 v = entry[f, pl.ds(re * CH + at, 16), :] * inverse[re] * gain
@@ -293,17 +318,17 @@
                 for d, (p, q) in enumerate(((0, 1), (3, 4), (1, 2))):
                     for part, source in enumerate((his, los, his)):
                         rows = pl.ds((part * 3 + d) * CH + at, 16)
-                        xs[w, rows, 0:128] = source[p]
-                        xs[w, rows, 128:256] = source[q]
+                        xs[f, w, rows, 0:128] = source[p]
+                        xs[f, w, rows, 128:256] = source[q]
             return 0
 
-        lax.fori_loop(0, CH // 16, group, 0)
+        lax.fori_loop(0, CH // 16, group, 0, unroll=True)
 
     def middle_of(f):
         reach = min(3, FRAMES - f)
 
         def step(w, _):
-            y = dot(u[w, 0 : reach * CH, :], xs[w])
+            y = dot(u[w, 0 : reach * CH, :], xs[f, w])
             for later in range(reach):
                 part = y[later * CH : (later + 1) * CH]
                 if f == 0 or later == 2:
@@ -312,35 +337,35 @@
                     sums[f + later, w] = sums[f + later, w] + part
             return 0
 
-        lax.fori_loop(0, 6, step, 0)
+        lax.fori_loop(0, 6, step, 0, unroll=True)
 
     def latent_of(f):
         def group(i, totals):
-            at = pl.multiple_of(i * 16, 16)
-            bias = cols[pl.ds(at, 16), 6:7]
+            at = i * 16
+            bias = wide_column(1, at)
             y = [sums[f, w, pl.ds(at, 16), :] for w in range(6)]
             s12, d12, s34, d34 = y[1] + y[2], y[1] - y[2], y[3] + y[4], y[3] - y[4]
             made = (y[0] + s12 + s34, d12 + 2 * d34, s12 + 4 * s34, d12 + 8 * d34 + y[5])
             fresh = []
             for r in range(4):
                 v = entry[f, pl.ds((r + 1) * CH + at, 16), :] + bias + made[r]
-                mixed[r, pl.ds(at, 16), :] = v
+                mixed[f, r, pl.ds(at, 16), :] = v
                 fresh.append(totals[r] + v * v)
             return tuple(fresh)
 
         zero = jnp.zeros((16, LANES), F32)
-        totals = lax.fori_loop(0, CH // 16, group, (zero,) * 4)
+        totals = lax.fori_loop(0, CH // 16, group, (zero,) * 4, unroll=True)
         inverse = [
             lax.rsqrt(jnp.sum(x, axis=0, keepdims=True) * (1 / CH) + EPSILON) for x in totals
         ]
         side = pl.ds(f % 2 * 128, 128)
 
         def finish(i, _):
-            at = pl.multiple_of(i * 16, 16)
-            gain = cols[pl.ds(at, 16), 7:8] * 0.5
+            at = i * 16
+            gain = wide_column(2, at)
             act = []
             for r in range(4):
-                v = mixed[r, pl.ds(at, 16), :] * inverse[r] * gain
+                v = mixed[f, r, pl.ds(at, 16), :] * inverse[r] * gain
                 act.append(v + v * jnp.tanh(v))
             for r in range(2):
                 for pair in range(2):
@@ -351,25 +376,27 @@
                     for c, x in ((2 * pair, even), (2 * pair + 1, odd)):
                         hi, lo = halves(x)
                         rows = pl.ds((c * 2 + r) * CH + at, 16)
-                        zs[0, rows, side] = hi
-                        zs[1, rows, side] = lo
+                        zs[f // 2, 0, rows, side] = hi
+                        zs[f // 2, 1, rows, side] = lo
             return 0
 
-        lax.fori_loop(0, CH // 16, finish, 0)
+        lax.fori_loop(0, CH // 16, finish, 0, unroll=True)
 
     def tokens_of(f):
-        both = dot(wb[...], zs[0])
-        bias = jnp.concatenate([cols[:, 8:9], cols[0:32, 9:10]], axis=0)
-        made = both[0:128] + both[128:256] + dot(wb[0:128], zs[1]) + bias
-        turned[...] = jnp.transpose(made)
+        both = dot(wb[...], zs[f // 2, 0])
+        bias = jnp.concatenate([end[...], end[...]], axis=1)
+        made = both[0:128] + both[128:256] + dot(wb[0:128], zs[f // 2, 1]) + bias
+        turned[f // 2] = jnp.transpose(made)
         for side in range(2):
             for clip in range(CLIPS):
                 for t in range(13):
                     rows = pl.ds(side * 128 + clip * 16 + t + 1, 2, stride=64)
-                    out[clip * 4 + f - 1 + side, :, pl.ds(t * 128, 128)] = turned[rows, :]
-
+                    out[clip * 4 + f - 1 + side, :, pl.ds(t * 128, 128)] = turned[f // 2, rows, :]
+
+    entry_of(0)
     for f in range(FRAMES):
-        entry_of(f)
+        if f + 1 < FRAMES:
+            entry_of(f + 1)
         middle_of(f)
         latent_of(f)
         if f % 2:
@@ -384,20 +411,28 @@
     shape((6, 3 * CH, MID_K), BF16),
     shape((6 * CH, 3 * LANES), BF16),
     shape((256, 8 * CH), BF16),
-    shape((CH, 128), F32),
+    shape((3, CH, 128), F32),
     shape((CH, LANES), F32),
+    shape((128, 128), F32),
 )
+VMEM_BYTES = 60 * 2**20
 VMEM = pl.BlockSpec(memory_space=pltpu.VMEM)
-SMEM = pl.BlockSpec(memory_space=pltpu.SMEM)
+HBM = pl.BlockSpec(memory_space=pltpu.HBM)
 ENCODE_SCRATCH = [
     pltpu.VMEM((FRAMES * LANES, LANES), BF16),
     pltpu.VMEM((FRAMES, 6 * CH, LANES), F32),
-    pltpu.VMEM((6, MID_K, LANES), BF16),
+    pltpu.VMEM((FRAMES, 6, MID_K, LANES), BF16),
     pltpu.VMEM((FRAMES, 6, CH, LANES), F32),
-    pltpu.VMEM((4, CH, LANES), F32),
-    pltpu.VMEM((2, 8 * CH, LANES), BF16),
-    pltpu.VMEM((LANES, 128), F32),
+    pltpu.VMEM((FRAMES, 4, CH, LANES), F32),
+    pltpu.VMEM((2, 2, 8 * CH, LANES), BF16),
+    pltpu.VMEM((2, LANES, 128), F32),
 ]
+
+
+def whole_kernel(*refs):
+    args, out, (made, exchange, encode) = refs[:12], refs[12], refs[13:]
+    exchange_kernel(*args, *made, *exchange)
+    encode_kernel(where_am_i, *made, out, *encode)
 
 
 def where_am_i():
@@ -411,36 +446,45 @@
     def line(x):
         return x.reshape(1, -1)
 
-    video, *made = pl.pallas_call(
-        exchange_kernel,
-        out_shape=(shape((NF, 24, 128), F32),) + MADE,
-        in_specs=[VMEM, SMEM, SMEM] + [VMEM] * 9,
-        out_specs=(pl.BlockSpec(memory_space=pl.ANY),) + (VMEM,) * 5,
+    return pl.pallas_call(
+        whole_kernel,
+        out_shape=shape((NF, 2, TILE), F32),
+        in_specs=[HBM] * 12,
+        out_specs=VMEM,
         scratch_shapes=[
-            pltpu.VMEM((128, TILE), F32),
-            pltpu.VMEM((24, TILE + 256), F32),
-            pltpu.VMEM((N_SEQ, 24, 128), F32),
-            pltpu.SemaphoreType.DMA((16,)),
-            pltpu.SemaphoreType.DMA((16,)),
-            pltpu.SemaphoreType.DMA((16,)),
-            pltpu.SemaphoreType.DMA((16,)),
-            pltpu.SemaphoreType.DMA,
+            [pltpu.VMEM((NF, 24, 128), F32)] + [pltpu.VMEM(x.shape, x.dtype) for x in MADE],
+            [
+                pltpu.VMEM((6, 1, TILE), F32),
+                pltpu.SMEM((1, 6), I32),
+                pltpu.SMEM((4,), I32),
+                pltpu.VMEM((81, CH), F32),
+                pltpu.VMEM((1, CH), F32),
+                pltpu.VMEM((4, CH), F32),
+                pltpu.VMEM((1, CH), F32),
+                pltpu.VMEM((27, CH, CH), F32),
+                pltpu.VMEM((1, CH), F32),
+                pltpu.VMEM((1, CH), F32),
+                pltpu.VMEM((ZCH, CH), F32),
+                pltpu.VMEM((1, ZCH), F32),
+                pltpu.SemaphoreType.DMA((12,)),
+                pltpu.VMEM((128, TILE), F32),
+                pltpu.VMEM((24, TILE + 256), F32),
+                pltpu.VMEM((N_SEQ, 24, 128), F32),
+                pltpu.SemaphoreType.DMA((16,)),
+                pltpu.SemaphoreType.DMA((16,)),
+                pltpu.SemaphoreType.DMA((16,)),
+                pltpu.SemaphoreType.DMA((16,)),
+                pltpu.SemaphoreType.DMA,
+            ],
+            ENCODE_SCRATCH,
         ],
         compiler_params=pltpu.CompilerParams(
-            collective_id=0, has_side_effects=True, vmem_limit_bytes=40 * 2**20
+            collective_id=0, has_side_effects=True, vmem_limit_bytes=VMEM_BYTES
         ),
     )(
-        loaded, tile_rows, bucket_ids, in_weight, line(in_bias), bucket_bias, line(norm_gain),
+        jnp.transpose(loaded, (1, 0, 2)), tile_rows, bucket_ids, in_weight.T, line(in_bias), bucket_bias, line(norm_gain),
         mid_weight, line(mid_bias), line(head_gain), head_weight, line(head_bias),
     )
-    return pl.pallas_call(
-        functools.partial(encode_kernel, where_am_i),
-        out_shape=shape((NF, 2, TILE), F32),
-        in_specs=[VMEM] * 6,
-        out_specs=VMEM,
-        scratch_shapes=ENCODE_SCRATCH,
-        compiler_params=pltpu.CompilerParams(vmem_limit_bytes=48 * 2**20),
-    )(video, *made)
 
 
 def solution(mesh):

time: 59.9 us -> 37.4 us (0.62)
  Pallas kernels: 50.6 us -> 35.6 us
  local copies, waits for them, and re-layouts: 8.94 us -> 1.63 us
    pallas_call x2 -> x1, Pallas kernels: 50.6 us -> 35.6 us  [body(): pl.pallas_call(whole_kernel, out_shape=shape((NF, 2, TILE), F32), in_spec...]
    unnamed x22 -> x1, local copies, waits for them, and re-layouts: 8.94 us -> 1.63 us
where the time goes in v2:
time: 37.4 us; the launch traced here: 37.2 us
  Pallas kernels  35.6 us (95%)
  local copies, waits for them, and re-layouts  1.63 us (4%)
    pallas_call x1, Pallas kernels, body(): pl.pallas_call(whole_kernel, out_shape=shape((NF, 2, TILE), F32), in_spec...  35.6 us
    unnamed x1, local copies, waits for them, and re-layouts  1.63 us

profile of v2, /device:TPU:1, one launch (start us, length us, event | category | flops | bytes accessed | tf_op | source)
XLA Modules:
  0.0 37.2 jit_solution(17126781530332907293)
XLA Ops:
  0.0 35.6 %shard_map.118 = f32[16,2,1664]{2,1,0:T(2,128)} custom-call(f32[6,1,1664]{2,1,0:T(1,128)} %bitcast.8, s32[1,6]{1,0:T(1,128)} %refs_1_.1, s32[4]{0:T(128)} %refs_2_.1, f32[81,96]{1,0:T(8,128)} %bitcast.7, f32[1,96]{1,0:T(1,128)} %bitcast.9, f32[4,96]{1,0:T(4,128)} %refs_5_.1, f32[1,96]{1,0:T(1,128)} %bitcast.10, f32[27,96,96]{2,1,0:T(8,128)} %refs_7_.1, ...), custom_call_target="tpu_custom_call" | custom-call | tf_op jit(solution)/shard_map/pallas_call | solution.py:449
  35.6 1.6 %copy.14 = f32[16,2,1664]{2,1,0:T(2,128)} copy(f32[16,2,1664]{2,1,0:T(2,128)} %shard_map.118) | data formatting | bytes 425984

commit v3 on v2

--- a/solution.py
+++ b/solution.py
@@ -22,6 +22,10 @@
 TILE = 2 * W
 LANES = 256
 MID_K = 9 * CH
+PIECES = (0, 6, 7, 1, 8, 2, 9, 3, 10, 4, 11, 5, 12)
+CHUNKS = ((0, 31), (31, 24), (55, 24))
+WINDOWS = (4, 5, 7)
+
 
 G43 = (
     (1 / 4, 0.0, 0.0),
@@ -144,28 +148,28 @@
 
     loads[0].wait()
     loads[1].wait()
-    here = pl.ds(pl.multiple_of(o * 8, 8), 8)
-    lane = iota((1, TILE), 1)
-    numbers = jnp.full((1, TILE), -1000.0, F32)
+    lane = iota((1, 128), 1)
+    numbers = jnp.full((1, 128), -1000.0, F32)
     for j in range(6):
         numbers = jnp.where(lane == 8 * o + j, numbers_smem[0, j].astype(F32), numbers)
-    got[here, :] = jnp.concatenate(
-        [raw[j] for j in range(6)] + [numbers, jnp.zeros((1, TILE), F32)], axis=0
-    )
+        for at, t in enumerate(PIECES):
+            got[o, pl.ds(1 + 6 * at + j, 1), :] = raw[j, :, t * 128 : t * 128 + 128]
+    got[o, 0:1, :] = numbers
+    picked[:, 0:128] = jnp.zeros((16, 128), F32)
+    picked[:, 128 + TILE :] = jnp.zeros((16, 128), F32)
     pl.semaphore_wait(barrier, 30)
 
-    first = []
-    for k in range(1, 16):
-        copy = pltpu.make_async_remote_copy(
-            src_ref=got.at[here],
-            dst_ref=got.at[here],
-            send_sem=send1.at[k],
-            recv_sem=recv1.at[k],
-            device_id=(lax.rem(o + k, 16), g),
-            device_id_type=MESH,
-        )
-        copy.start()
-        first.append(copy)
+    for c, (start, rows) in enumerate(CHUNKS):
+        part = got.at[o, pl.ds(start, rows)]
+        for k in range(1, 16):
+            pltpu.make_async_remote_copy(
+                src_ref=part,
+                dst_ref=part,
+                send_sem=send1,
+                recv_sem=recv1.at[c],
+                device_id=(lax.rem(o + k, 16), g),
+                device_id_type=MESH,
+            ).start()
 
     for load in loads[2:]:
         load.wait()
@@ -174,59 +178,62 @@
         bias_head, u, we, wb, cols, off, end,
     )
 
-    for copy in first:
-        copy.wait()
-
-    label = got[pl.ds(6, 1), 0:128]
-    for l in range(1, 16):
-        label = jnp.maximum(label, got[pl.ds(8 * l + 6, 1), 0:128])
-    m = iota((24, 128), 0) % 12
-    pg, c = m // 3, m % 3
-    wanted = 6 * o + 6 * ((pg + 1) // 2 - 1) + 2 * c + (pg + 1) % 2
-    hot = jnp.where(label == wanted.astype(F32), 1.0, 0.0).astype(BF16)
-    hot2 = jnp.concatenate([hot, hot], axis=1)
-    picked[:, 0:128] = jnp.zeros((24, 128), F32)
-    picked[:, 128 + TILE :] = jnp.zeros((24, 128), F32)
-    for at in range(0, TILE, 128):
-        hi, lo = halves(got[:, at : at + 128])
-        picked[:, 128 + at : 256 + at] = dot(hot2, jnp.concatenate([hi, lo], axis=0))
-
-    half = lax.rem(g // FRAMES, 2) * 64
-    lane = iota((8, 128), 1) - half
-    inside = (lane >= 0) & (lane < 64)
-    upper = iota((8, 128), 0) < 4
-    for s in range(N_SEQ):
-        col = lane + (COLS * s - 4)
-        keep = inside & (col >= 0) & (col < W)
-        pieces = []
-        for h, rows in ((0, 0), (0, 8), (1, 8), (1, 16)):
-            start = 128 + h * W + COLS * s - 4
-            base = start // 128 * 128
-            wide = picked[rows : rows + 8, base : base + 256]
-            turned = pltpu.roll(wide, lax.rem(half + 256 - (start - base), 256), 1)
-            pieces.append(turned[:, 0:128])
-        sent[s, 0:8] = jnp.where(keep, pieces[0], 0.0)
-        sent[s, 8:16] = jnp.where(keep, jnp.where(upper, pieces[1], pieces[2]), 0.0)
-        sent[s, 16:24] = jnp.where(keep, pieces[3], 0.0)
-
-    second = []
-    for k in range(1, 16):
-        s = lax.rem(g + k, 16)
-        copy = pltpu.make_async_remote_copy(
-            src_ref=sent.at[s],
-            dst_ref=video.at[g],
-            send_sem=send2.at[k],
-            recv_sem=recv2.at[k],
-            device_id=(o, s),
-            device_id_type=MESH,
-        )
-        copy.start()
-        second.append(copy)
-    own = pltpu.make_async_copy(sent.at[g], video.at[g], own_sem)
+    lane = iota((16, 128), 1)
+    hot2 = None
+    done = 0
+    for c, (start, rows) in enumerate(CHUNKS):
+        wait_for(got.at[pl.ds(0, 15), pl.ds(start, rows)], recv1.at[c])
+        if c == 0:
+            label = got[0, 0:1, :]
+            for l in range(1, 16):
+                label = jnp.maximum(label, got[l, 0:1, :])
+            m = iota((16, 128), 0)
+            pg, colour = m // 3, m % 3
+            wanted = 6 * o + 6 * ((pg + 1) // 2 - 1) + 2 * colour + (pg + 1) % 2
+            hot = jnp.where((label == wanted.astype(F32)) & (m < 12), 1.0, 0.0).astype(BF16)
+            hot2 = jnp.concatenate([hot, hot], axis=1)
+        for at in range(max(start - 1, 0) // 6, (start + rows - 1) // 6):
+            pieces = []
+            for l in range(16):
+                pieces += [got[l, pl.ds(1 + 6 * at, 6), :], jnp.zeros((2, 128), F32)]
+            hi, lo = halves(jnp.concatenate(pieces, axis=0))
+            column = 128 * (PIECES[at] + 1)
+            picked[:, column : column + 128] = dot(hot2, jnp.concatenate([hi, lo], axis=0))
+        count = WINDOWS[c]
+        for s in range(done, done + count):
+            col = lane % 64 + (COLS * s - 4)
+            keep = (col >= 0) & (col < W)
+            pieces = []
+            for h in range(2):
+                first = 128 + h * W + COLS * s - 4
+                at = first // 128 * 128
+                turned = pltpu.roll(picked[:, at : at + 256], (h * 64 - (first - at)) % 256, 1)
+                pieces.append(turned[:, 0:128])
+            both = jnp.where(lane < 64, pieces[0], pieces[1])
+            sent[s] = jnp.where(keep, both, 0.0)
+        for k in range(count):
+            s = done + lax.rem(g + k, count)
+
+            @pl.when(s != g)
+            def _():
+                pltpu.make_async_remote_copy(
+                    src_ref=sent.at[s, pl.ds(0, 12)],
+                    dst_ref=video.at[g, pl.ds(0, 12)],
+                    send_sem=send2,
+                    recv_sem=recv2,
+                    device_id=(o, s),
+                    device_id_type=MESH,
+                ).start()
+
+        done += count
+    own = pltpu.make_async_copy(sent.at[g, pl.ds(0, 12)], video.at[g, pl.ds(0, 12)], own_sem)
     own.start()
     own.wait()
-    for copy in second:
-        copy.wait()
+    wait_for(video.at[pl.ds(0, 15), pl.ds(0, 12)], recv2)
+
+
+def wait_for(ref, sem):
+    pltpu.make_async_copy(ref, ref, sem).wait()
 
 
 def encode_kernel(
@@ -240,15 +247,15 @@
     in_frame = jnp.where((col >= 0) & (col < W), 1.0, 0.0)
     low = iota((16, 128), 1) < 64
 
-    low8 = iota((24, 128), 1) < 64
+    low12 = iota((12, 128), 1) < 64
     lines = []
     for f in range(FRAMES):
+        blocks = [video[4 * clip + f, 0:12, :] for clip in range(CLIPS)]
+        flipped = [pltpu.roll(x, 64, 1) for x in blocks]
+        first = [jnp.where(low12, blocks[c], flipped[c + 1]) for c in (0, 2)]
+        second = [jnp.where(low12, flipped[c], blocks[c + 1]) for c in (0, 2)]
         wide = jnp.concatenate(
-            [
-                jnp.where(low8, video[f], video[4 + f]),
-                jnp.where(low8, video[8 + f], video[12 + f]),
-            ],
-            axis=1,
+            [jnp.concatenate(first, axis=1), jnp.concatenate(second, axis=1)], axis=0
         )
         hi = wide.astype(BF16).astype(F32)
         lines += [hi, wide - hi]
@@ -433,6 +440,9 @@
     args, out, (made, exchange, encode) = refs[:12], refs[12], refs[13:]
     exchange_kernel(*args, *made, *exchange)
     encode_kernel(where_am_i, *made, out, *encode)
+    got, _, sent, send1, _, send2 = exchange[13:19]
+    wait_for(got.at[pl.ds(0, 15), pl.ds(0, 79)], send1)
+    wait_for(sent.at[pl.ds(0, 15), pl.ds(0, 12)], send2)
 
 
 def where_am_i():
@@ -452,7 +462,7 @@
         in_specs=[HBM] * 12,
         out_specs=VMEM,
         scratch_shapes=[
-            [pltpu.VMEM((NF, 24, 128), F32)] + [pltpu.VMEM(x.shape, x.dtype) for x in MADE],
+            [pltpu.VMEM((NF, 16, 128), F32)] + [pltpu.VMEM(x.shape, x.dtype) for x in MADE],
             [
                 pltpu.VMEM((6, 1, TILE), F32),
                 pltpu.SMEM((1, 6), I32),
@@ -467,13 +477,13 @@
                 pltpu.VMEM((ZCH, CH), F32),
                 pltpu.VMEM((1, ZCH), F32),
                 pltpu.SemaphoreType.DMA((12,)),
-                pltpu.VMEM((128, TILE), F32),
-                pltpu.VMEM((24, TILE + 256), F32),
-                pltpu.VMEM((N_SEQ, 24, 128), F32),
-                pltpu.SemaphoreType.DMA((16,)),
-                pltpu.SemaphoreType.DMA((16,)),
-                pltpu.SemaphoreType.DMA((16,)),
-                pltpu.SemaphoreType.DMA((16,)),
+                pltpu.VMEM((16, 80, 128), F32),
+                pltpu.VMEM((16, TILE + 256), F32),
+                pltpu.VMEM((N_SEQ, 16, 128), F32),
+                pltpu.SemaphoreType.DMA,
+                pltpu.SemaphoreType.DMA((3,)),
+                pltpu.SemaphoreType.DMA,
+                pltpu.SemaphoreType.DMA,
                 pltpu.SemaphoreType.DMA,
             ],
             ENCODE_SCRATCH,

time: 37.4 us -> 30.1 us (0.80)
  Pallas kernels: 35.6 us -> 28.3 us
    pallas_call x1, Pallas kernels: 35.6 us -> 28.3 us  [body(): pl.pallas_call(whole_kernel, out_shape=shape((NF, 2, TILE), F32), in_spec...]
where the time goes in v3:
time: 30.1 us; the launch traced here: 29.9 us
  Pallas kernels  28.3 us (94%)
  local copies, waits for them, and re-layouts  1.63 us (5%)
    pallas_call x1, Pallas kernels, body(): pl.pallas_call(whole_kernel, out_shape=shape((NF, 2, TILE), F32), in_spec...  28.3 us
    unnamed x1, local copies, waits for them, and re-layouts  1.63 us

profile of v3, /device:TPU:1, one launch (start us, length us, event | category | flops | bytes accessed | tf_op | source)
XLA Modules:
  0.0 29.9 jit_solution(7697631044035617172)
XLA Ops:
  0.0 28.3 %shard_map.118 = f32[16,2,1664]{2,1,0:T(2,128)} custom-call(f32[6,1,1664]{2,1,0:T(1,128)} %bitcast.8, s32[1,6]{1,0:T(1,128)} %refs_1_.1, s32[4]{0:T(128)} %refs_2_.1, f32[81,96]{1,0:T(8,128)} %bitcast.7, f32[1,96]{1,0:T(1,128)} %bitcast.9, f32[4,96]{1,0:T(4,128)} %refs_5_.1, f32[1,96]{1,0:T(1,128)} %bitcast.10, f32[27,96,96]{2,1,0:T(8,128)} %refs_7_.1, ...), custom_call_target="tpu_custom_call" | custom-call | tf_op jit(solution)/shard_map/pallas_call | solution.py:459
  28.3 1.6 %copy.14 = f32[16,2,1664]{2,1,0:T(2,128)} copy(f32[16,2,1664]{2,1,0:T(2,128)} %shard_map.118) | data formatting | bytes 425984

commit v4 on v3

--- a/solution.py
+++ b/solution.py
@@ -52,7 +52,7 @@
 
 def prepare(
     ids, in_weight, in_bias, bucket_bias, norm_gain, mid_weight, mid_bias, head_gain,
-    head_weight, head_bias, u, we, wb, cols, off, end,
+    head_weight, head_bias, u, we, wb, cols, end,
 ):
     for a in range(3):
         for d in range(3):
@@ -80,6 +80,20 @@
     first = n < 216
     k = iota((81, LANES), 0)
     whi, wlo = halves(jnp.transpose(in_weight[...]))
+    lines = jnp.concatenate(
+        [in_bias[...], bucket_bias[...], norm_gain[...], mid_bias[...], head_gain[...]], axis=0
+    )
+    table = jnp.transpose(lines)
+    lane = iota((CH, LANES), 1)
+    offsets = jnp.zeros((CH, LANES), F32)
+    for c in range(CLIPS):
+        rest = table[:, 0:1] + sum(
+            table[:, 1 + b : 2 + b] * jnp.where(ids[c] == b, 1.0, 0.0) for b in range(4)
+        )
+        for i in range(3):
+            piece = rest.astype(BF16).astype(F32)
+            offsets = jnp.where(lane == 216 + 3 * c + i, piece, offsets)
+            rest = rest - piece
     for re in range(6):
         b = row - re
         legal = first & (b >= 0) & (b <= 2)
@@ -88,21 +102,11 @@
             e01 = jnp.where(hit & (part < 2), 1.0, 0.0).astype(BF16)
             e2 = jnp.where(hit & (part == 2), 1.0, 0.0).astype(BF16)
             got = dot(whi, e01) + dot(wlo, e2)
+            if a == 2:
+                got = got + offsets
             we[pl.ds(re * CH, CH), pl.ds(a * LANES, LANES)] = got.astype(BF16)
-    lines = jnp.concatenate(
-        [in_bias[...], bucket_bias[...], norm_gain[...], mid_bias[...], head_gain[...]], axis=0
-    )
-    table = jnp.transpose(lines)
     for i, (at, scale) in enumerate(((5, 0.5), (6, 1.0), (7, 0.5))):
         cols[i] = jnp.broadcast_to(table[:, at : at + 1] * scale, (CH, 128))
-    clip = iota((CH, LANES), 1) % 64 // 16
-    total = jnp.broadcast_to(table[:, 0:1], (CH, LANES))
-    for c in range(CLIPS):
-        mine = sum(
-            table[:, 1 + b : 2 + b] * jnp.where(ids[c] == b, 1.0, 0.0) for b in range(4)
-        )
-        total = total + jnp.where(clip == c, mine, 0.0)
-    off[...] = total
     line = iota((128, ZCH), 0)
     spread = jnp.where(line % 64 // 4 == iota((128, ZCH), 1), 1.0, 0.0)
     hhi, hlo = halves(head_weight[...])
@@ -122,7 +126,7 @@
 def exchange_kernel(
     loaded, tile_rows, bucket_ids, in_weight, in_bias, bucket_bias, norm_gain, mid_weight, mid_bias,
     head_gain, head_weight, head_bias,
-    video, u, we, wb, cols, off, end,
+    video, u, we, wb, cols, end,
     raw, numbers_smem, ids, weight_in, bias_in, buckets, gain1, weight_mid, bias_mid, gain2,
     weight_head, bias_head, in_sems,
     got, picked, sent, send1, recv1, send2, recv2, own_sem,
@@ -175,7 +179,7 @@
         load.wait()
     prepare(
         ids, weight_in, bias_in, buckets, gain1, weight_mid, bias_mid, gain2, weight_head,
-        bias_head, u, we, wb, cols, off, end,
+        bias_head, u, we, wb, cols, end,
     )
 
     lane = iota((16, 128), 1)
@@ -237,7 +241,7 @@
 
 
 def encode_kernel(
-    position, video, u, we, wb, cols, off, end,
+    position, video, u, we, wb, cols, end,
     out, x3, entry, xs, sums, mixed, zs, turned,
 ):
     o, s = position()
@@ -277,6 +281,9 @@
         right = jnp.where(select, b32, b0s)
         return left, middle, right
 
+    which_clip = jnp.where(
+        iota((40, LANES), 0) // 3 == iota((40, LANES), 1) % 64 // 16, 1.0, 0.0
+    )
     for f in range(FRAMES):
         block = placed[48 * f : 48 * f + 48]
         v0, v1 = block[:, 0:128], block[:, 128:256]
@@ -285,19 +292,22 @@
         for a, b in ((left, middle), (v0, v1), (middle, right)):
             both = jnp.concatenate([a, b], axis=1)
             taps += [both, both[0:24]]
-        taps.append(jnp.zeros((40, LANES), F32))
+        taps.append(which_clip)
         x3[pl.ds(f * LANES, LANES), :] = jnp.concatenate(taps, axis=0).astype(BF16)
 
-    def entry_of(f):
+    scales = {}
+
+    def entry_dot(f):
         first = max(0, f - 2)
         k0 = (2 - (f - first)) * LANES
         entry[f] = dot(we[:, k0:], x3[pl.ds(first * LANES, (f - first + 1) * LANES), :])
+
+    def entry_norm(f):
         inverse = []
         for re in range(6):
             total = jnp.zeros((8, LANES), F32)
             for c in range(0, CH, 8):
-                value = entry[f, pl.ds(re * CH + c, 8), :] + off[pl.ds(c, 8), :]
-                entry[f, pl.ds(re * CH + c, 8), :] = value
+                value = entry[f, pl.ds(re * CH + c, 8), :]
                 total = total + value * value
             mean = jnp.sum(total, axis=0, keepdims=True) * (1 / CH)
             scale = lax.rsqrt(mean + EPSILON) * in_frame
@@ -306,8 +316,11 @@
             if re == 5:
                 scale = scale * jnp.where(o < N_DP - 1, 1.0, 0.0)
             inverse.append(scale)
-
-        def group(i, _):
+        scales[f] = inverse
+
+    def active_of(f):
+        def group(i):
+            inverse = scales[f]
             at = i * 16
             gain = wide_column(0, at)
             act = []
@@ -327,14 +340,13 @@
                         rows = pl.ds((part * 3 + d) * CH + at, 16)
                         xs[f, w, rows, 0:128] = source[p]
                         xs[f, w, rows, 128:256] = source[q]
-            return 0
-
-        lax.fori_loop(0, CH // 16, group, 0, unroll=True)
+
+        return [functools.partial(group, i) for i in range(CH // 16)]
 
     def middle_of(f):
         reach = min(3, FRAMES - f)
 
-        def step(w, _):
+        def step(w):
             y = dot(u[w, 0 : reach * CH, :], xs[f, w])
             for later in range(reach):
                 part = y[later * CH : (later + 1) * CH]
@@ -342,12 +354,13 @@
                     sums[f + later, w] = part
                 else:
                     sums[f + later, w] = sums[f + later, w] + part
-            return 0
-
-        lax.fori_loop(0, 6, step, 0, unroll=True)
-
-    def latent_of(f):
-        def group(i, totals):
+
+        return [functools.partial(step, w) for w in range(6)]
+
+    squares = {}
+
+    def mixed_of(f):
+        def group(i):
             at = i * 16
             bias = wide_column(1, at)
             y = [sums[f, w, pl.ds(at, 16), :] for w in range(6)]
@@ -357,17 +370,21 @@
             for r in range(4):
                 v = entry[f, pl.ds((r + 1) * CH + at, 16), :] + bias + made[r]
                 mixed[f, r, pl.ds(at, 16), :] = v
-                fresh.append(totals[r] + v * v)
-            return tuple(fresh)
-
-        zero = jnp.zeros((16, LANES), F32)
-        totals = lax.fori_loop(0, CH // 16, group, (zero,) * 4, unroll=True)
-        inverse = [
-            lax.rsqrt(jnp.sum(x, axis=0, keepdims=True) * (1 / CH) + EPSILON) for x in totals
-        ]
+                fresh.append(v * v + squares[f][r] if i else v * v)
+            squares[f] = fresh
+
+        return [functools.partial(group, i) for i in range(CH // 16)]
+
+    def latent_of(f):
         side = pl.ds(f % 2 * 128, 128)
 
-        def finish(i, _):
+        def group(i):
+            if i == 0:
+                squares[f] = [
+                    lax.rsqrt(jnp.sum(x, axis=0, keepdims=True) * (1 / CH) + EPSILON)
+                    for x in squares[f]
+                ]
+            inverse = squares[f]
             at = i * 16
             gain = wide_column(2, at)
             act = []
@@ -385,9 +402,8 @@
                         rows = pl.ds((c * 2 + r) * CH + at, 16)
                         zs[f // 2, 0, rows, side] = hi
                         zs[f // 2, 1, rows, side] = lo
-            return 0
-
-        lax.fori_loop(0, CH // 16, finish, 0, unroll=True)
+
+        return [functools.partial(group, i) for i in range(CH // 16)]
 
     def tokens_of(f):
         both = dot(wb[...], zs[f // 2, 0])
@@ -400,14 +416,28 @@
                     rows = pl.ds(side * 128 + clip * 16 + t + 1, 2, stride=64)
                     out[clip * 4 + f - 1 + side, :, pl.ds(t * 128, 128)] = turned[f // 2, rows, :]
 
-    entry_of(0)
-    for f in range(FRAMES):
-        if f + 1 < FRAMES:
-            entry_of(f + 1)
-        middle_of(f)
-        latent_of(f)
-        if f % 2:
-            tokens_of(f)
+    def beside(main, *others):
+        rest = [task for tasks in others for task in tasks]
+        for i, task in enumerate(main):
+            task()
+            for other in rest[i * len(rest) // len(main) : (i + 1) * len(rest) // len(main)]:
+                other()
+
+    def run(f, task):
+        return [functools.partial(task, f)]
+
+    entry_dot(0)
+    entry_dot(1)
+    entry_norm(0)
+    beside(active_of(0), run(2, entry_dot), run(1, entry_norm))
+    beside(middle_of(0), active_of(1), run(3, entry_dot), run(2, entry_norm))
+    beside(middle_of(1), active_of(2), mixed_of(0), latent_of(0), run(3, entry_norm))
+    beside(middle_of(2), active_of(3), mixed_of(1), latent_of(1))
+    beside(middle_of(3), run(1, tokens_of), mixed_of(2), latent_of(2))
+    for tasks in (mixed_of(3), latent_of(3)):
+        for task in tasks:
+            task()
+    tokens_of(3)
 
 
 def shape(dims, dtype):
@@ -419,10 +449,9 @@
     shape((6 * CH, 3 * LANES), BF16),
     shape((256, 8 * CH), BF16),
     shape((3, CH, 128), F32),
-    shape((CH, LANES), F32),
     shape((128, 128), F32),
 )
-VMEM_BYTES = 60 * 2**20
+VMEM_BYTES = 48 * 2**20
 VMEM = pl.BlockSpec(memory_space=pltpu.VMEM)
 HBM = pl.BlockSpec(memory_space=pltpu.HBM)
 ENCODE_SCRATCH = [
@@ -456,9 +485,14 @@
     def line(x):
         return x.reshape(1, -1)
 
+    operands = (
+        jnp.transpose(loaded, (1, 0, 2)), tile_rows, bucket_ids, in_weight.T, line(in_bias),
+        bucket_bias, line(norm_gain), mid_weight, line(mid_bias), line(head_gain), head_weight,
+        line(head_bias),
+    )
     return pl.pallas_call(
         whole_kernel,
-        out_shape=shape((NF, 2, TILE), F32),
+        out_shape=pltpu.VMEM((NF, 2, TILE), F32),
         in_specs=[HBM] * 12,
         out_specs=VMEM,
         scratch_shapes=[
@@ -491,10 +525,7 @@
         compiler_params=pltpu.CompilerParams(
             collective_id=0, has_side_effects=True, vmem_limit_bytes=VMEM_BYTES
         ),
-    )(
-        jnp.transpose(loaded, (1, 0, 2)), tile_rows, bucket_ids, in_weight.T, line(in_bias), bucket_bias, line(norm_gain),
-        mid_weight, line(mid_bias), line(head_gain), head_weight, line(head_bias),
-    )
+    )(*[pltpu.with_memory_space_constraint(x, pltpu.HBM) for x in operands])
 
 
 def solution(mesh):

time: 30.1 us -> 28.1 us (0.934)
  Pallas kernels: 28.3 us -> 27.3 us
  local copies, waits for them, and re-layouts: 1.63 us -> 0.69 us
    pallas_call x1, Pallas kernels: 28.3 us -> 27.3 us  [body(): pl.pallas_call(whole_kernel, out_shape=pltpu.VMEM((NF, 2, TILE), F32), in...]
    unnamed x1, local copies, waits for them, and re-layouts: 1.63 us -> 0.69 us
where the time goes in v4:
time: 28.1 us; the launch traced here: 28 us
  Pallas kernels  27.3 us (97%)
  local copies, waits for them, and re-layouts  0.69 us (2%)
    pallas_call x1, Pallas kernels, body(): pl.pallas_call(whole_kernel, out_shape=pltpu.VMEM((NF, 2, TILE), F32), in...  27.3 us
    unnamed x1, local copies, waits for them, and re-layouts  0.69 us

profile of v4, /device:TPU:1, one launch (start us, length us, event | category | flops | bytes accessed | tf_op | source)
XLA Modules:
  0.0 28.0 jit_solution(2583117971661890289)
XLA Ops:
  0.0 27.3 %shard_map.118 = f32[16,2,1664]{2,1,0:T(2,128)S(1)} custom-call(f32[6,1,1664]{2,1,0:T(1,128)} %bitcast.8, s32[1,6]{1,0:T(1,128)} %refs_1_.1, s32[4]{0:T(128)} %refs_2_.1, f32[81,96]{1,0:T(8,128)} %bitcast.7, f32[1,96]{1,0:T(1,128)} %bitcast.9, f32[4,96]{1,0:T(4,128)} %refs_5_.1, f32[1,96]{1,0:T(1,128)} %bitcast.10, f32[27,96,96]{2,1,0:T(8,128)} %refs_7_.1, ...), custom_call_target="tpu_custom_call" | custom-call | tf_op jit(solution)/shard_map/pallas_call | solution.py:493
  27.3 0.7 %copy.14 = f32[16,2,1664]{2,1,0:T(2,128)} copy(f32[16,2,1664]{2,1,0:T(2,128)S(1)} %shard_map.118) | data formatting | bytes 425984

commit v5 on v4

--- a/solution.py
+++ b/solution.py
@@ -132,6 +132,10 @@
     got, picked, sent, send1, recv1, send2, recv2, own_sem,
 ):
     o, g = lax.axis_index("dp"), lax.axis_index("seq")
+    barrier = pltpu.get_barrier_semaphore()
+    for k in range(1, 16):
+        pl.semaphore_signal(barrier, 1, device_id=(lax.rem(o + k, 16), g), device_id_type=MESH)
+        pl.semaphore_signal(barrier, 1, device_id=(o, lax.rem(g + k, 16)), device_id_type=MESH)
     sources = (
         loaded, tile_rows, bucket_ids, in_weight, in_bias, bucket_bias, norm_gain, mid_weight,
         mid_bias, head_gain, head_weight, head_bias,
@@ -145,11 +149,6 @@
     ]
     for load in loads:
         load.start()
-    barrier = pltpu.get_barrier_semaphore()
-    for k in range(1, 16):
-        pl.semaphore_signal(barrier, 1, device_id=(lax.rem(o + k, 16), g), device_id_type=MESH)
-        pl.semaphore_signal(barrier, 1, device_id=(o, lax.rem(g + k, 16)), device_id_type=MESH)
-
     loads[0].wait()
     loads[1].wait()
     lane = iota((1, 128), 1)
@@ -252,8 +251,15 @@
     low = iota((16, 128), 1) < 64
 
     low12 = iota((12, 128), 1) < 64
-    lines = []
-    for f in range(FRAMES):
+    k = iota((LANES, LANES), 0)
+    j = iota((LANES, LANES), 1)
+    source = j % 64 // 16 * 64 + 4 * (j % 16) + j // 64
+    permute = jnp.where(k == source, 1.0, 0.0).astype(BF16)
+    which_clip = jnp.where(
+        iota((40, LANES), 0) // 3 == iota((40, LANES), 1) % 64 // 16, 1.0, 0.0
+    )
+
+    def pixels_of(f):
         blocks = [video[4 * clip + f, 0:12, :] for clip in range(CLIPS)]
         flipped = [pltpu.roll(x, 64, 1) for x in blocks]
         first = [jnp.where(low12, blocks[c], flipped[c + 1]) for c in (0, 2)]
@@ -262,30 +268,7 @@
             [jnp.concatenate(first, axis=1), jnp.concatenate(second, axis=1)], axis=0
         )
         hi = wide.astype(BF16).astype(F32)
-        lines += [hi, wide - hi]
-    k = iota((LANES, LANES), 0)
-    j = iota((LANES, LANES), 1)
-    source = j % 64 // 16 * 64 + 4 * (j % 16) + j // 64
-    permute = jnp.where(k == source, 1.0, 0.0).astype(BF16)
-    placed = dot(jnp.concatenate(lines, axis=0).astype(BF16), permute)
-
-    def wide_column(which, at):
-        column = cols[which, pl.ds(at, 16), :]
-        return jnp.concatenate([column, column], axis=1)
-
-    def shifted(v0, v1, select):
-        b10, b32 = pltpu.roll(v0, 64, 1), pltpu.roll(v1, 64, 1)
-        b3s, b0s = pltpu.roll(v1, 65, 1), pltpu.roll(v0, 63, 1)
-        left = jnp.where(select, b3s, b10)
-        middle = jnp.where(select, b10, b32)
-        right = jnp.where(select, b32, b0s)
-        return left, middle, right
-
-    which_clip = jnp.where(
-        iota((40, LANES), 0) // 3 == iota((40, LANES), 1) % 64 // 16, 1.0, 0.0
-    )
-    for f in range(FRAMES):
-        block = placed[48 * f : 48 * f + 48]
+        block = dot(jnp.concatenate([hi, wide - hi], axis=0).astype(BF16), permute)
         v0, v1 = block[:, 0:128], block[:, 128:256]
         left, middle, right = shifted(v0, v1, iota((48, 128), 1) < 64)
         taps = []
@@ -294,6 +277,18 @@
             taps += [both, both[0:24]]
         taps.append(which_clip)
         x3[pl.ds(f * LANES, LANES), :] = jnp.concatenate(taps, axis=0).astype(BF16)
+
+    def wide_column(which, at):
+        column = cols[which, pl.ds(at, 16), :]
+        return jnp.concatenate([column, column], axis=1)
+
+    def shifted(v0, v1, select):
+        b10, b32 = pltpu.roll(v0, 64, 1), pltpu.roll(v1, 64, 1)
+        b3s, b0s = pltpu.roll(v1, 65, 1), pltpu.roll(v0, 63, 1)
+        left = jnp.where(select, b3s, b10)
+        middle = jnp.where(select, b10, b32)
+        right = jnp.where(select, b32, b0s)
+        return left, middle, right
 
     scales = {}
 
@@ -405,16 +400,18 @@
 
         return [functools.partial(group, i) for i in range(CH // 16)]
 
-    def tokens_of(f):
-        both = dot(wb[...], zs[f // 2, 0])
-        bias = jnp.concatenate([end[...], end[...]], axis=1)
-        made = both[0:128] + both[128:256] + dot(wb[0:128], zs[f // 2, 1]) + bias
-        turned[f // 2] = jnp.transpose(made)
-        for side in range(2):
+    def tokens_of(first, count):
+        lanes = pl.ds(first % 2 * 128, count * 128)
+        part = [zs[first // 2, i, :, lanes] for i in range(2)]
+        both = dot(wb[...], part[0])
+        bias = jnp.concatenate([end[...]] * count, axis=1)
+        made = both[0:128] + both[128:256] + dot(wb[0:128], part[1]) + bias
+        turned[first // 2, lanes, :] = jnp.transpose(made)
+        for f in range(first, first + count):
             for clip in range(CLIPS):
                 for t in range(13):
-                    rows = pl.ds(side * 128 + clip * 16 + t + 1, 2, stride=64)
-                    out[clip * 4 + f - 1 + side, :, pl.ds(t * 128, 128)] = turned[f // 2, rows, :]
+                    rows = pl.ds(f % 2 * 128 + clip * 16 + t + 1, 2, stride=64)
+                    out[clip * 4 + f, :, pl.ds(t * 128, 128)] = turned[first // 2, rows, :]
 
     def beside(main, *others):
         rest = [task for tasks in others for task in tasks]
@@ -426,18 +423,23 @@
     def run(f, task):
         return [functools.partial(task, f)]
 
+    pixels_of(0)
     entry_dot(0)
+    pixels_of(1)
     entry_dot(1)
     entry_norm(0)
-    beside(active_of(0), run(2, entry_dot), run(1, entry_norm))
-    beside(middle_of(0), active_of(1), run(3, entry_dot), run(2, entry_norm))
+    pixels_of(2)
+    pixels_of(3)
+    beside(active_of(0), run(2, entry_dot), run(3, entry_dot), run(1, entry_norm))
+    beside(middle_of(0), active_of(1), run(2, entry_norm))
     beside(middle_of(1), active_of(2), mixed_of(0), latent_of(0), run(3, entry_norm))
     beside(middle_of(2), active_of(3), mixed_of(1), latent_of(1))
-    beside(middle_of(3), run(1, tokens_of), mixed_of(2), latent_of(2))
+    beside(middle_of(3), mixed_of(2), latent_of(2), [functools.partial(tokens_of, 0, 2)])
+    tokens_of(2, 1)
     for tasks in (mixed_of(3), latent_of(3)):
         for task in tasks:
             task()
-    tokens_of(3)
+    tokens_of(3, 1)
 
 
 def shape(dims, dtype):

time: 28.1 us -> 27.6 us (0.982)
  Pallas kernels: 27.3 us -> 26.9 us
    pallas_call x1, Pallas kernels: 27.3 us -> 26.9 us  [body(): pl.pallas_call(whole_kernel, out_shape=pltpu.VMEM((NF, 2, TILE), F32), in...]
where the time goes in v5:
time: 27.6 us; the launch traced here: 27.5 us
  Pallas kernels  26.9 us (97%)
  local copies, waits for them, and re-layouts  0.69 us (2%)
    pallas_call x1, Pallas kernels, body(): pl.pallas_call(whole_kernel, out_shape=pltpu.VMEM((NF, 2, TILE), F32), in...  26.9 us
    unnamed x1, local copies, waits for them, and re-layouts  0.69 us

profile of v5, /device:TPU:1, one launch (start us, length us, event | category | flops | bytes accessed | tf_op | source)
XLA Modules:
  0.0 27.5 jit_solution(15954398208325462486)
XLA Ops:
  0.0 26.9 %shard_map.118 = f32[16,2,1664]{2,1,0:T(2,128)S(1)} custom-call(f32[6,1,1664]{2,1,0:T(1,128)} %bitcast.8, s32[1,6]{1,0:T(1,128)} %refs_1_.1, s32[4]{0:T(128)} %refs_2_.1, f32[81,96]{1,0:T(8,128)} %bitcast.7, f32[1,96]{1,0:T(1,128)} %bitcast.9, f32[4,96]{1,0:T(4,128)} %refs_5_.1, f32[1,96]{1,0:T(1,128)} %bitcast.10, f32[27,96,96]{2,1,0:T(8,128)} %refs_7_.1, ...), custom_call_target="tpu_custom_call" | custom-call | tf_op jit(solution)/shard_map/pallas_call | solution.py:495
  26.9 0.7 %copy.14 = f32[16,2,1664]{2,1,0:T(2,128)} copy(f32[16,2,1664]{2,1,0:T(2,128)S(1)} %shard_map.118) | data formatting | bytes 425984

commit v6 on v5

--- a/solution.py
+++ b/solution.py
@@ -25,6 +25,8 @@
 PIECES = (0, 6, 7, 1, 8, 2, 9, 3, 10, 4, 11, 5, 12)
 CHUNKS = ((0, 31), (31, 24), (55, 24))
 WINDOWS = (4, 5, 7)
+FAR_SEQ = (8, 9, 7, 6, 10, 5, 11, 4, 12, 3, 13, 2, 14, 1, 15)
+FAR_DP = (10, 6, 9, 11, 14, 2, 8, 5, 7, 13, 15, 1, 3, 4, 12)
 
 
 G43 = (
@@ -133,9 +135,10 @@
 ):
     o, g = lax.axis_index("dp"), lax.axis_index("seq")
     barrier = pltpu.get_barrier_semaphore()
-    for k in range(1, 16):
+    for k in FAR_SEQ:
+        pl.semaphore_signal(barrier, 1, device_id=(o, lax.rem(g + k, 16)), device_id_type=MESH)
+    for k in FAR_DP:
         pl.semaphore_signal(barrier, 1, device_id=(lax.rem(o + k, 16), g), device_id_type=MESH)
-        pl.semaphore_signal(barrier, 1, device_id=(o, lax.rem(g + k, 16)), device_id_type=MESH)
     sources = (
         loaded, tile_rows, bucket_ids, in_weight, in_bias, bucket_bias, norm_gain, mid_weight,
         mid_bias, head_gain, head_weight, head_bias,

time: 27.6 us -> 27.6 us (level)
  no operation moved by 1% of the time
where the time goes in v6:
time: 27.6 us; the launch traced here: 27.5 us
  Pallas kernels  26.8 us (97%)
  local copies, waits for them, and re-layouts  0.69 us (2%)
    pallas_call x1, Pallas kernels, body(): pl.pallas_call(whole_kernel, out_shape=pltpu.VMEM((NF, 2, TILE), F32), in...  26.8 us
    unnamed x1, local copies, waits for them, and re-layouts  0.69 us

profile of v6, /device:TPU:1, one launch (start us, length us, event | category | flops | bytes accessed | tf_op | source)
XLA Modules:
  0.0 27.5 jit_solution(13749480546879558698)
XLA Ops:
  0.0 26.8 %shard_map.118 = f32[16,2,1664]{2,1,0:T(2,128)S(1)} custom-call(f32[6,1,1664]{2,1,0:T(1,128)} %bitcast.8, s32[1,6]{1,0:T(1,128)} %refs_1_.1, s32[4]{0:T(128)} %refs_2_.1, f32[81,96]{1,0:T(8,128)} %bitcast.7, f32[1,96]{1,0:T(1,128)} %bitcast.9, f32[4,96]{1,0:T(4,128)} %refs_5_.1, f32[1,96]{1,0:T(1,128)} %bitcast.10, f32[27,96,96]{2,1,0:T(8,128)} %refs_7_.1, ...), custom_call_target="tpu_custom_call" | custom-call | tf_op jit(solution)/shard_map/pallas_call | solution.py:498
  26.9 0.7 %copy.14 = f32[16,2,1664]{2,1,0:T(2,128)} copy(f32[16,2,1664]{2,1,0:T(2,128)S(1)} %shard_map.118) | data formatting | bytes 425984

commit v7 on v6

--- a/solution.py
+++ b/solution.py
@@ -334,7 +334,7 @@
                 left, middle, right = shifted(v0, v1, low)
                 his, los = zip(*[halves(x) for x in (left, middle, right, v0, v1)])
                 for d, (p, q) in enumerate(((0, 1), (3, 4), (1, 2))):
-                    for part, source in enumerate((his, los, his)):
+                    for part, source in enumerate((his, los)):
                         rows = pl.ds((part * 3 + d) * CH + at, 16)
                         xs[f, w, rows, 0:128] = source[p]
                         xs[f, w, rows, 128:256] = source[q]
@@ -345,7 +345,8 @@
         reach = min(3, FRAMES - f)
 
         def step(w):
-            y = dot(u[w, 0 : reach * CH, :], xs[f, w])
+            both = jnp.concatenate([xs[f, w], xs[f, w, 0 : 3 * CH]], axis=0)
+            y = dot(u[w, 0 : reach * CH, :], both)
             for later in range(reach):
                 part = y[later * CH : (later + 1) * CH]
                 if f == 0 or later == 2:
@@ -462,7 +463,7 @@
 ENCODE_SCRATCH = [
     pltpu.VMEM((FRAMES * LANES, LANES), BF16),
     pltpu.VMEM((FRAMES, 6 * CH, LANES), F32),
-    pltpu.VMEM((FRAMES, 6, MID_K, LANES), BF16),
+    pltpu.VMEM((FRAMES, 6, 6 * CH, LANES), BF16),
     pltpu.VMEM((FRAMES, 6, CH, LANES), F32),
     pltpu.VMEM((FRAMES, 4, CH, LANES), F32),
     pltpu.VMEM((2, 2, 8 * CH, LANES), BF16),

time: 27.6 us -> 27.6 us (level)
  no operation moved by 1% of the time
where the time goes in v7:
time: 27.6 us; the launch traced here: 27.5 us
  Pallas kernels  26.8 us (97%)
  local copies, waits for them, and re-layouts  0.69 us (2%)
    pallas_call x1, Pallas kernels, body(): pl.pallas_call(whole_kernel, out_shape=pltpu.VMEM((NF, 2, TILE), F32), in...  26.8 us
    unnamed x1, local copies, waits for them, and re-layouts  0.69 us

profile of v7, /device:TPU:1, one launch (start us, length us, event | category | flops | bytes accessed | tf_op | source)
XLA Modules:
  0.0 27.5 jit_solution(13749480546879558698)
XLA Ops:
  0.0 26.8 %shard_map.118 = f32[16,2,1664]{2,1,0:T(2,128)S(1)} custom-call(f32[6,1,1664]{2,1,0:T(1,128)} %bitcast.8, s32[1,6]{1,0:T(1,128)} %refs_1_.1, s32[4]{0:T(128)} %refs_2_.1, f32[81,96]{1,0:T(8,128)} %bitcast.7, f32[1,96]{1,0:T(1,128)} %bitcast.9, f32[4,96]{1,0:T(4,128)} %refs_5_.1, f32[1,96]{1,0:T(1,128)} %bitcast.10, f32[27,96,96]{2,1,0:T(8,128)} %refs_7_.1, ...), custom_call_target="tpu_custom_call" | custom-call | tf_op jit(solution)/shard_map/pallas_call | solution.py:499
  26.9 0.7 %copy.14 = f32[16,2,1664]{2,1,0:T(2,128)} copy(f32[16,2,1664]{2,1,0:T(2,128)S(1)} %shard_map.118) | data formatting | bytes 425984
